TPU v7x, 256 devices: a whole 4x4x8 slice. The times are simulated.
256 devices in a mesh: leaf: 32 (over y, z), panel: 8 (over x, core).
Axes of the slice: x: 4, y: 4, z: 8, core: 2. Of those that a mesh axis runs over, the one named last changes fastest.
Arguments:
- rhs_sub: float32 [256, 512, 256], P(('leaf', 'panel')), may hold values from -6 to 6
- rhs_sep: float32 [3, 2048, 256], P(None, ('leaf', 'panel')), may hold values from -6 to 6
- sub_factor: float32 [256, 512, 512], P(('leaf', 'panel')), may hold values from -0.25 to 0.25
- sub_diag: float32 [256, 512], P(('leaf', 'panel')), may hold values from 1 to 2
- sep_factor: float32 [2048, 3584], P(('leaf', 'panel')), may hold values from -0.1875 to 0.1875
- sep_diag: float32 [3, 2048], P(None, ('leaf', 'panel')), may hold values from 1 to 2
- sub_update: float32 [256, 1792, 512], P(('leaf', 'panel')), may hold values from -6 to 6
- update_rows: int32 [256, 1792], P(('leaf', 'panel')), may hold values from 0 to 2047, as said below
- sep_update: float32 [256, 5120, 8], P(('leaf', 'panel')), may hold values from -6 to 6
Outputs:
- solution_sub: float32 [256, 512, 256], P(('leaf', 'panel'))
- solution_sep: float32 [3, 2048, 256], P(None, ('leaf', 'panel'))
Inputs may be any that keep to these rules, and one draw needn't show every extreme that they name: Within each level's part of a row of update_rows the entries are distinct rows of that level's node, fewer than the node's row count, and the node's last row is always among them.
All inputs are finite; a program needn't handle non-finite values.
Results may differ from a plain program's by a relative error of at most 0.0003.
Values sent between devices are 32-bit elements; how exact they have to be, the bound alone decides.
A program may use at most 128 MiB of HBM per device.

v0:
```python
import jax
import jax.numpy as jnp
from jax import lax
from jax.sharding import PartitionSpec as P


def swapped(shard, axis, bit):
    return lax.ppermute(shard, axis, [(i, i ^ 1 << bit) for i in range(lax.axis_size(axis))])


def sub_offset(target, total_rows):
    return sum((total_rows // 2**inner_level // 2 for inner_level in range(target)))


def sep_offset(source, target, total_rows):
    offset_value = 0
    for earlier in range(1, source):
        offset_value += sum((total_rows // 2**inner_level for inner_level in range(earlier)))
    return offset_value + sum((total_rows // 2**inner_level for inner_level in range(target)))


def column_offset(target, total_rows):
    return sum((total_rows // 2**inner_level for inner_level in range(target)))


def weight_scale(target, group_size, local_rows, levels, total_rows):
    fan_total = group_size // 2**target * local_rows // 2 + (levels - 1 - target) * (
        total_rows // 2**target
    )
    return float(fan_total) ** (-0.5)


def triangle(strict, diagonal):
    order_size = strict.shape[-1]
    return jnp.tril(strict, -1) + diagonal[..., :, None] * jnp.eye(order_size, dtype=jnp.float32)


def solve_lower(matrix, right_side, transposed):
    return lax.linalg.triangular_solve(
        matrix, right_side, left_side=True, lower=True, transpose_a=transposed
    )


def halving(partial_value, group_bits, position):
    for bit_index in reversed(range(group_bits)):
        half_rows = partial_value.shape[0] // 2
        lower_half = partial_value[:half_rows]
        upper_half = partial_value[half_rows:]
        is_upper = position >> bit_index & 1 == 1
        retained = jnp.where(is_upper, upper_half, lower_half)
        handed = jnp.where(is_upper, lower_half, upper_half)
        partial_value = retained + swapped(handed, "leaf", bit_index)
    return partial_value


def doubling(gathered_rows, group_bits, position):
    for bit_index in range(group_bits):
        partner = swapped(gathered_rows, "leaf", bit_index)
        is_upper = position >> bit_index & 1 == 1
        gathered_rows = jnp.where(
            is_upper,
            jnp.concatenate([partner, gathered_rows], axis=0),
            jnp.concatenate([gathered_rows, partner], axis=0),
        )
    return gathered_rows


def sectioned_sum(partial_value, group_bits, leaf_position):
    shares = lax.psum_scatter(partial_value, "panel", scatter_dimension=0, tiled=True)
    shares = doubling(halving(shares, group_bits, leaf_position), group_bits, leaf_position)
    return lax.all_gather(shares, "panel", axis=0, tiled=True)


def body(
    rhs_sub,
    rhs_sep,
    sub_factor,
    sub_diag,
    sep_factor,
    sep_diag,
    sub_update,
    update_rows,
    sep_update,
):
    precise = lax.Precision.HIGHEST
    contract_first = (((0,), (0,)), ((), ()))
    group_size = lax.axis_size(("leaf", "panel"))
    leaf_bits = lax.axis_size("leaf").bit_length() - 1
    leaf_position = lax.axis_index("leaf")
    position = lax.axis_index(("leaf", "panel"))
    levels = sep_diag.shape[0]
    block_rows = sep_diag.shape[1]
    local_rows = sub_factor.shape[1]
    total_rows = block_rows * group_size
    sub_lower = triangle(sub_factor[0], sub_diag[0])

    def node_sum(partial_value, target):
        if target == 0:
            return sectioned_sum(partial_value, leaf_bits, leaf_position)
        return sectioned_sum(partial_value, leaf_bits - target, leaf_position)

    inverse_rows = []
    own_starts = []
    for target in range(levels):
        node_rows = total_rows >> target
        own_start = position % (group_size >> target) * block_rows
        column_start = column_offset(target, total_rows)
        strict = sep_factor[:, column_start : column_start + node_rows]
        row_ids = own_start + lax.broadcasted_iota(jnp.int32, (block_rows, node_rows), 0)
        col_ids = lax.broadcasted_iota(jnp.int32, (block_rows, node_rows), 1)
        lower_part = jnp.where(col_ids < row_ids, strict, 0.0)
        diagonal_part = jnp.where(col_ids == row_ids, sep_diag[target][:, None], 0.0)
        inverse_rows.append(lower_part + diagonal_part)
        own_starts.append(own_start)
    right_sub = rhs_sub[0]
    columns = right_sub.shape[1]
    sub_solved = solve_lower(sub_lower, right_sub, False)
    solved = [None] * levels
    for target in reversed(range(levels)):
        node_rows = total_rows >> target
        offset_sub = sub_offset(target, total_rows)
        coupling = sub_update[0, offset_sub : offset_sub + node_rows // 2]
        rows_used = update_rows[0, offset_sub : offset_sub + node_rows // 2]
        partial_value = (
            jnp.zeros((node_rows, columns), jnp.float32)
            .at[rows_used]
            .add(jnp.dot(coupling, sub_solved, precision=precise))
        )
        for source in range(target + 1, levels):
            offset_sep = sep_offset(source, target, total_rows)
            partial_value = partial_value + jnp.dot(
                sep_update[0, offset_sep : offset_sep + node_rows],
                solved[source],
                precision=precise,
            )
        level_scale = weight_scale(target, group_size, local_rows, levels, total_rows)
        negated = level_scale * partial_value
        own_rows = (
            lax.dynamic_slice_in_dim(negated, own_starts[target], block_rows, 0) - rhs_sep[target]
        )
        negated = lax.dynamic_update_slice_in_dim(negated, own_rows, own_starts[target], 0)
        everything = node_sum(negated, target)
        solved[target] = jnp.dot(inverse_rows[target], -everything, precision=precise)
    finished = [None] * levels
    own_results = []
    for target in range(levels):
        current = solved[target]
        for ancestor in range(target):
            offset_sep = sep_offset(target, ancestor, total_rows)
            coupling_block = sep_update[0, offset_sep : offset_sep + (total_rows >> ancestor)]
            ancestor_scale = weight_scale(ancestor, group_size, local_rows, levels, total_rows)
            current = current - ancestor_scale * lax.dot_general(
                coupling_block, finished[ancestor], contract_first, precision=precise
            )
        terms = lax.dot_general(inverse_rows[target], current, contract_first, precision=precise)
        finished[target] = node_sum(terms, target)
        own_results.append(
            lax.dynamic_slice_in_dim(finished[target], own_starts[target], block_rows, 0)
        )
    current_sub = sub_solved
    for target in range(levels):
        node_rows = total_rows >> target
        offset_sub = sub_offset(target, total_rows)
        picked = finished[target][update_rows[0, offset_sub : offset_sub + node_rows // 2]]
        level_scale = weight_scale(target, group_size, local_rows, levels, total_rows)
        current_sub = current_sub - level_scale * lax.dot_general(
            sub_update[0, offset_sub : offset_sub + node_rows // 2],
            picked,
            contract_first,
            precision=precise,
        )
    result_sub = solve_lower(sub_lower, current_sub, True)
    result_sep = jnp.stack(own_results)
    return (result_sub[None], result_sep)


def solution(mesh):
    in_specs = (
        P(("leaf", "panel"), None, None),
        P(None, ("leaf", "panel"), None),
        P(("leaf", "panel"), None, None),
        P(("leaf", "panel"), None),
        P(("leaf", "panel"), None),
        P(None, ("leaf", "panel")),
        P(("leaf", "panel"), None, None),
        P(("leaf", "panel"), None),
        P(("leaf", "panel"), None, None),
    )
    out_specs = (P(("leaf", "panel"), None, None), P(None, ("leaf", "panel"), None))
    return jax.shard_map(body, mesh=mesh, in_specs=in_specs, out_specs=out_specs, check_vma=False)
```

profile of v0, /device:TPU:1, one launch (start us, length us, event | category | flops | bytes accessed | tf_op | source)
XLA Modules:
  0.0 749.3 jit_solution(4387121192410164495)
XLA Ops:
  8.8 8.0 %while.1 = (s32[]{:T(128)}, f32[512,512]{1,0:T(8,128)S(1)}, s32[4,2]{0,1:T(2,128)S(1)}, f32[4,128,128]{2,1,0:T(8,128)S(1)}, s32[]{:T(128)}) while((s32[]{:T(128)}, f32[512,512]{1,0:T(8,128)S(1)}, s32[4,2]{0,1:T(2,128)S(1)}, f32[4,128,128]{2,1,0:T(8,128)S(1)}, s32[]{:T(128)}) %tuple.25), condition=%wide.while_cond, body=%wide.while_body.sunk | while | flops 2 | bytes 131181 | solution.py:39
  16.8 39.3 %custom-call.5 = f32[4,128,128]{1,2,0:T(8,128)S(1)} custom-call(f32[4,128,128]{2,1,0:T(8,128)S(1)} %get-tuple-element.9), custom_call_target="InvertDiagBlocksLowerTriangular" | custom-call | tf_op jit(solution)/shard_map/triangular_solve | solution.py:39
  58.4 2.1 convolution_bitcast_fusion.2
  64.4 35.0 %reduce-scatter.7.cloned.1.call-done = f32[64,256]{1,0:T(8,128)} async-done(((f32[512,256]{1,0:T(8,128)}), f32[64,256]{1,0:T(8,128)}) %reduce-scatter.7.cloned.1.call-update) | async-done | bytes 65552 | tf_op jit(solution)/shard_map/reduce_scatter | solution.py:69
  100.2 5.2 collective-permute-start
  107.8 2.4 collective-permute-start.1
  112.3 3.1 convolution_bitcast_fusion.1
  118.1 2.3 collective-permute-start.4
  121.6 5.1 collective-permute-start.5
  128.5 22.8 %all_gather.18 = f32[512,256]{1,0:T(8,128)S(1)} all-gather(f32[64,256]{1,0:T(8,128)S(1)} %maximum_select_fusion.6), channel_id=1, replica_groups=mesh['leaf'=32,'panel'=8] {'panel'}, dimensions={0}, use_global_device_ids=true | all-gather | bytes 589824 | tf_op jit(solution)/shard_map/all_gather | solution.py:71
  154.5 3.7 scatter_fusion
  160.1 30.9 %reduce-scatter.9.cloned.1.call-done = f32[128,256]{1,0:T(8,128)} async-done(((f32[1024,256]{1,0:T(8,128)}), f32[128,256]{1,0:T(8,128)}) %reduce-scatter.9.cloned.1.call-update) | async-done | bytes 131088 | tf_op jit(solution)/shard_map/reduce_scatter | solution.py:69
  192.9 2.2 collective-permute-done.6
  196.0 5.3 collective-permute-start.7
  202.8 2.6 collective-permute-start.8
  212.2 2.4 collective-permute-start.11
  215.7 5.1 collective-permute-start.12
  226.8 5.1 fusion.9
  232.9 30.1 %all-gather.5.cloned.1.call-done = f32[1024,256]{1,0:T(8,128)} async-done(((f32[128,256]{1,0:T(8,128)}), f32[1024,256]{1,0:T(8,128)}) %all-gather.5.cloned.1.call-update) | async-done | bytes 1048592 | tf_op jit(solution)/shard_map/all_gather | solution.py:71
  266.6 3.1 fusion
  271.7 6.9 scatter_fusion.1
  281.5 33.2 %reduce-scatter.11.cloned.1.call-done = f32[256,256]{1,0:T(8,128)} async-done(((f32[2048,256]{1,0:T(8,128)}), f32[256,256]{1,0:T(8,128)}) %reduce-scatter.11.cloned.1.call-update) | async-done | bytes 262160 | tf_op jit(solution)/shard_map/reduce_scatter | solution.py:69
  315.7 2.6 collective-permute-start.14
  318.2 2.8 collective-permute-done.14
  323.2 2.3 collective-permute-done.15
  325.6 5.5 collective-permute-start.16
  332.5 2.6 collective-permute-start.17
  341.5 2.3 collective-permute-start.20
  345.0 5.5 collective-permute-start.21
  353.2 2.1 collective-permute-done.22
  355.4 3.1 collective-permute-start.23
  358.5 2.4 collective-permute-done.23
  361.6 40.9 %all-gather.7.cloned.1.call-done = f32[2048,256]{1,0:T(8,128)} async-done(((f32[256,256]{1,0:T(8,128)}), f32[2048,256]{1,0:T(8,128)}) %all-gather.7.cloned.1.call-update) | async-done | bytes 2097168 | tf_op jit(solution)/shard_map/all_gather | solution.py:71
  402.6 2.6 fusion.5
  405.1 3.3 fusion.89
  408.4 33.6 %reduce-scatter.13.cloned.1.call-done = f32[256,256]{1,0:T(8,128)} async-done(((f32[2048,256]{1,0:T(8,128)}), f32[256,256]{1,0:T(8,128)}) %reduce-scatter.13.cloned.1.call-update) | async-done | bytes 262160 | tf_op jit(solution)/shard_map/reduce_scatter | solution.py:69
  443.1 2.6 collective-permute-start.24
  445.6 2.8 collective-permute-done.24
  450.5 2.4 collective-permute-done.25
  452.9 5.5 collective-permute-start.26
  459.8 2.6 collective-permute-start.27
  468.9 2.2 collective-permute-start.30
  472.4 5.3 collective-permute-start.31
  480.4 2.1 collective-permute-done.32
  482.6 3.4 collective-permute-start.33
  485.9 2.4 collective-permute-done.33
  489.3 40.7 %all-gather.9.cloned.1.call-done = f32[2048,256]{1,0:T(8,128)} async-done(((f32[256,256]{1,0:T(8,128)}), f32[2048,256]{1,0:T(8,128)}) %all-gather.9.cloned.1.call-update) | async-done | bytes 2097168 | tf_op jit(solution)/shard_map/all_gather | solution.py:71
  530.0 2.7 fusion.30
  532.7 2.1 fusion.100
  534.9 32.0 %reduce-scatter.15.cloned.1.call-done = f32[128,256]{1,0:T(8,128)} async-done(((f32[1024,256]{1,0:T(8,128)}), f32[128,256]{1,0:T(8,128)}) %reduce-scatter.15.cloned.1.call-update) | async-done | bytes 131088 | tf_op jit(solution)/shard_map/reduce_scatter | solution.py:69
  571.9 5.3 collective-permute-start.35
  578.8 2.4 collective-permute-start.36
  591.6 4.5 collective-permute-start.40
  596.1 2.2 collective-permute-done.40
  603.5 35.4 %all-gather.11.cloned.1.call-done = f32[1024,256]{1,0:T(8,128)} async-done(((f32[128,256]{1,0:T(8,128)}), f32[1024,256]{1,0:T(8,128)}) %all-gather.11.cloned.1.call-update) | async-done | bytes 1048592 | tf_op jit(solution)/shard_map/all_gather | solution.py:71
  642.3 30.7 %reduce-scatter.17.cloned.1.call-done = f32[64,256]{1,0:T(8,128)} async-done(((f32[512,256]{1,0:T(8,128)}), f32[64,256]{1,0:T(8,128)}) %reduce-scatter.17.cloned.1.call-update) | async-done | bytes 65552 | tf_op jit(solution)/shard_map/reduce_scatter | solution.py:69
  673.8 5.3 collective-permute-start.42
  681.4 2.4 collective-permute-start.43
  686.0 4.7 gather_fusion
  691.8 6.2 fusion.18
  697.9 2.2 collective-permute-start.46
  701.5 5.0 collective-permute-start.47
  708.2 21.3 %all_gather.23 = f32[512,256]{1,0:T(8,128)S(1)} all-gather(f32[64,256]{1,0:T(8,128)S(1)} %maximum_select_fusion.11), channel_id=1, replica_groups=mesh['leaf'=32,'panel'=8] {'panel'}, dimensions={0}, use_global_device_ids=true | all-gather | bytes 589824 | tf_op jit(solution)/shard_map/all_gather | solution.py:71
  732.6 3.0 fusion.23
  (277 shorter events, 134.8 us)
Async XLA Ops:
  7.2 92.3 %reduce-scatter.7.cloned.1.call-start = ((), (), s32[]{:S(2)}) async-start(), calls=%async_computation.6 | async-start | bytes 589824 | tf_op jit(solution)/shard_map/reduce_scatter | solution.py:69
  58.4 168.3 %copy-start.4 = (f32[128,256]{1,0:T(8,128)}, f32[128,256]{1,0:T(8,128)S(1)}, u32[]{:S(2)}) copy-start(f32[128,256]{1,0:T(8,128)S(1)} %fusion.84) | copy-start | bytes 393220
  64.4 126.6 %reduce-scatter.9.cloned.1.call-start = ((), (), s32[]{:S(2)}) async-start(), calls=%async_computation.7 | async-start | bytes 1179648 | tf_op jit(solution)/shard_map/reduce_scatter | solution.py:69
  100.2 6.8 collective-permute-start
  107.8 3.7 collective-permute-start.1
  111.5 4.0 collective-permute-start.2
  115.5 2.6 collective-permute-start.3
  118.1 3.5 collective-permute-start.4
  121.6 6.9 collective-permute-start.5
  160.0 102.9 %all-gather.5.cloned.1.call-start = ((), (), s32[]{:S(2)}) async-start(), calls=%async_computation.8 | async-start | bytes 1179648 | tf_op jit(solution)/shard_map/all_gather | solution.py:71
  191.9 3.2 collective-permute-start.6
  196.0 6.8 collective-permute-start.7
  202.8 4.0 collective-permute-start.8
  206.8 2.6 collective-permute-start.9
  209.4 2.8 collective-permute-start.10
  212.2 3.5 collective-permute-start.11
  215.7 6.7 collective-permute-start.12
  222.4 3.2 collective-permute-start.13
  226.3 88.4 %reduce-scatter.11.cloned.1.call-start = ((), (), s32[]{:S(2)}) async-start(), calls=%async_computation.9 | async-start | bytes 2359296 | tf_op jit(solution)/shard_map/reduce_scatter | solution.py:69
  281.4 121.1 %copy-start.12 = (f32[8,3584]{1,0:T(8,128)S(1)}, f32[8,3584]{1,0:T(8,128)}, u32[]{:S(2)}) copy-start(f32[8,3584]{1,0:T(8,128)} %param.13) | copy-start | bytes 344068
  281.4 121.1 %copy-start.21 = (f32[8]{0:T(128)S(1)}, f32[8]{0:T(128)}, u32[]{:S(2)}) copy-start(f32[8]{0:T(128)} %get-tuple-element.20) | copy-start | bytes 100
  281.5 121.1 %all-gather.7.cloned.1.call-start = ((), (), s32[]{:S(2)}) async-start(), calls=%async_computation.10 | async-start | bytes 2359296 | tf_op jit(solution)/shard_map/all_gather | solution.py:71
  315.7 5.4 collective-permute-start.14
  322.1 3.5 collective-permute-start.15
  325.6 6.9 collective-permute-start.16
  332.5 3.7 collective-permute-start.17
  336.2 2.8 collective-permute-start.18
  339.0 2.5 collective-permute-start.19
  341.5 3.5 collective-permute-start.20
  345.0 6.9 collective-permute-start.21
  351.9 3.5 collective-permute-start.22
  355.4 5.5 collective-permute-start.23
  361.6 80.5 %reduce-scatter.13.cloned.1.call-start = ((), (), s32[]{:S(2)}) async-start(), calls=%async_computation.11 | async-start | bytes 2359296 | tf_op jit(solution)/shard_map/reduce_scatter | solution.py:69
  408.4 121.7 %copy-start.10 = (f32[1,5120,8]{1,2,0:T(8,128)S(1)}, f32[1,5120,8]{1,2,0:T(8,128)}, u32[]{:S(2)}) copy-start(f32[1,5120,8]{1,2,0:T(8,128)} %param.17) | copy-start | bytes 491524
  408.4 121.6 %all-gather.9.cloned.1.call-start = ((), (), s32[]{:S(2)}) async-start(), calls=%async_computation.12 | async-start | bytes 2359296 | tf_op jit(solution)/shard_map/all_gather | solution.py:71
  443.1 5.4 collective-permute-start.24
  449.5 83.2 %copy-start.18 = (f32[8]{0:T(128)S(1)}, f32[8]{0:T(128)}, u32[]{:S(2)}) copy-start(f32[8]{0:T(128)} %get-tuple-element.22) | copy-start | bytes 100
  449.5 3.4 collective-permute-start.25
  452.9 6.9 collective-permute-start.26
  459.8 3.7 collective-permute-start.27
  463.6 2.8 collective-permute-start.28
  466.4 2.5 collective-permute-start.29
  468.9 3.5 collective-permute-start.30
  472.4 6.9 collective-permute-start.31
  479.2 3.3 collective-permute-start.32
  482.6 5.7 collective-permute-start.33
  489.0 77.9 %reduce-scatter.15.cloned.1.call-start = ((), (), s32[]{:S(2)}) async-start(), calls=%async_computation.13 | async-start | bytes 1179648 | tf_op jit(solution)/shard_map/reduce_scatter | solution.py:69
  534.8 104.1 %all-gather.11.cloned.1.call-start = ((), (), s32[]{:S(2)}) async-start(), calls=%async_computation.14 | async-start | bytes 1179648 | tf_op jit(solution)/shard_map/all_gather | solution.py:71
  567.8 3.2 collective-permute-start.34
  571.9 6.9 collective-permute-start.35
  578.8 3.9 collective-permute-start.36
  582.7 2.6 collective-permute-start.37
  585.3 2.8 collective-permute-start.38
  588.1 3.5 collective-permute-start.39
  591.6 6.8 collective-permute-start.40
  598.4 3.2 collective-permute-start.41
  602.3 83.7 %copy-start.15 = (s32[512,1]{0,1:T(1,128)S(1)}, s32[512,1]{0,1:T(1,128)}, u32[]{:S(2)}) copy-start(s32[512,1]{0,1:T(1,128)} %copy-done.14) | copy-start | bytes 6148
  602.3 70.7 %reduce-scatter.17.cloned.1.call-start = ((), (), s32[]{:S(2)}) async-start(), calls=%async_computation.15 | async-start | bytes 589824 | tf_op jit(solution)/shard_map/reduce_scatter | solution.py:69
  673.8 6.8 collective-permute-start.42
  681.4 3.8 collective-permute-start.43
  685.2 5.6 collective-permute-start.44
  690.7 7.2 collective-permute-start.45
  697.9 3.6 collective-permute-start.46
  701.5 6.7 collective-permute-start.47
  (23 other events, 912.0 us)
Sparse Core Ops, SparseCore 0:
  64.5 34.8 reduce-scatter.6
  160.1 30.8 reduce-scatter.8
  226.4 36.4 all-gather.4
  281.6 33.0 reduce-scatter.10
  361.7 40.7 all-gather.6
  408.5 33.5 reduce-scatter.12
  489.2 40.8 all-gather.8
  535.0 31.9 reduce-scatter.14
  602.4 36.4 all-gather.10
  642.4 30.5 reduce-scatter.16
where the time goes:
time: 759 us; the launch traced here: 749 us
  waiting for transfers between devices  417 us (55%)
  starting transfers between devices  125 us (16%)
  other arithmetic  73.7 us (10%)
  matrix products  53.3 us (7%)
  blocking collectives  44 us (6%)
  local copies, waits for them, and re-layouts  20.6 us (3%)
  between operations  15.6 us (2%)
    reduce_scatter x6, waiting for transfers between devices, sectioned_sum(): lax.psum_scatter(partial_value, 'panel', scatter_dimension=0, tiled=True)  195 us
    all_gather x4, waiting for transfers between devices, sectioned_sum(): return lax.all_gather(shares, 'panel', axis=0, tiled=True)  147 us
    ppermute x48, starting transfers between devices, swapped(): lax.ppermute(shard, axis, [(i, i ^ 1 << bit) for i in range(lax.axis_size...  124 us
    ppermute x48, waiting for transfers between devices, swapped(): lax.ppermute(shard, axis, [(i, i ^ 1 << bit) for i in range(lax.axis_size...  74.6 us
    all_gather x2, blocking collectives, sectioned_sum(): return lax.all_gather(shares, 'panel', axis=0, tiled=True)  44 us
    another operation x3, other arithmetic, solve_lower(): lax.linalg.triangular_solve(matrix, right_side, left_side=True, lower=Tru...  40.8 us
  transfers between devices with their start and end apart: 58, of which 55 were waited for; matrix products, arithmetic and copies ran while one was open for 3% of the time, Pallas kernels for 0%

commit v1 on v0

v1 whole, which is shorter than its diff:
```python
import functools

import jax
import jax.numpy as jnp
from jax import lax
from jax.experimental import pallas as pl
from jax.experimental.pallas import tpu as pltpu
from jax.sharding import PartitionSpec as P

MESH = pl.DeviceIdType.MESH
F32 = jnp.float32
BF16 = jnp.bfloat16
NN = (((1,), (0,)), ((), ()))
NT = (((1,), (1,)), ((), ()))
TN = (((0,), (0,)), ((), ()))

NX, NY, NZ = 4, 4, 8
ROWS, RHS, LOC, BLK = 2048, 256, 512, 8
LEVELS = 3
LANES = 128
COLS = 16
G2, E21, G1, E20, E10, G0, WIDE = 0, 512, 1536, 2560, 4608, 6656, 8704


def weight_scale(target):
    fan_total = (256 >> target) * LOC // 2 + (LEVELS - 1 - target) * (ROWS >> target)
    return float(fan_total) ** (-0.5)


def split(value):
    high = value.astype(BF16)
    return high, (value - high.astype(F32)).astype(BF16)


def small_dot(left, right, dims):
    left_high, left_low = split(left)
    right_high, right_low = split(right)
    rows = left.shape[0]
    both = jnp.concatenate([left_high, left_low], axis=0)
    first = lax.dot_general(both, right_high, dims, preferred_element_type=F32)
    second = lax.dot_general(left_high, right_low, dims, preferred_element_type=F32)
    return first[:rows] + first[rows:] + second


def place():
    leaf, panel = lax.axis_index("leaf"), lax.axis_index("panel")
    return panel // 2, leaf // NZ, leaf % NZ, panel % 2


def device(x, y, z, c):
    return (y * NZ + z, x * 2 + c)


def chain_kernel(
    ut0, ut1, ut2, m_ref, x0, x1, x2,
    b2c, b1c, b0c, b2x, b2s, b2z, b1x, b1s, b1y, b1t, b1z, b0y, b0s, b0x, b0t, b0z,
    g2, p1, p1r, g1, p0, p0r, g0, q0, q0r, h0, q1, q1r, h1, q2, q2r, h2,
    ssem, rsem,
):
    x, y, z, c = place()
    partner = y + 1 - 2 * (y % 2)
    yy = y % 2
    sibling = device(x, y, z, 1 - c)
    plane = [(a, b) for a in range(NX) for b in range(NY)][1:]
    half = [(a, b) for a in range(NX) for b in range(2)][1:]

    def xs(a):
        return (x + a) % NX

    def ys(b):
        return (y + b) % NY

    def zs(d):
        return (z + d) % NZ

    def pair_y(b):
        return partner if b else y

    barrier = pltpu.get_barrier_semaphore()
    greeted = [device(xs(a), ys(b), z, c) for a, b in plane]
    greeted += [device(x, y, zs(d), c) for d in range(1, NZ)] + [sibling]
    for peer in greeted:
        pl.semaphore_signal(barrier, inc=1, device_id=peer, device_id_type=MESH)
    pl.semaphore_wait(barrier, len(greeted))

    copies = []

    def send(src, dst, peer):
        at = len(copies)
        copy = pltpu.make_async_remote_copy(
            src_ref=src, dst_ref=dst, send_sem=ssem.at[at], recv_sem=rsem.at[at],
            device_id=peer, device_id_type=MESH,
        )
        copy.start()
        copies.append(copy)
        return copy

    def arrive(batch):
        for copy in batch:
            copy.wait_recv()

    mine = pl.ds(pl.multiple_of(c * LANES, LANES), LANES)
    other = pl.ds(pl.multiple_of((1 - c) * LANES, LANES), LANES)
    cols = pl.ds(pl.multiple_of(z * COLS, COLS), COLS)
    spread = pl.ds(pl.multiple_of(c * LANES + z * COLS, COLS), COLS)

    c2 = send(ut2.at[:, other, :], b2c, sibling)
    c1 = send(ut1.at[:, other, :], b1c, sibling)
    c0 = send(ut0.at[:, other, :], b0c, sibling)

    def add_own(total, own):
        def step(i, carry):
            total[i] = total[i] + own[i, mine, :]
            return carry

        lax.fori_loop(0, total.shape[0], step, 0)

    def z_stage(summed, parts):
        return [
            send(summed.at[pl.ds(pl.multiple_of(zs(d) * COLS, COLS), COLS), :], parts.at[d - 1], device(x, y, zs(d), c))
            for d in range(1, NZ)
        ]

    def z_sum(summed, parts, batch):
        arrive(batch)
        total = summed[cols, :]
        for d in range(NZ - 1):
            total = total + parts[d]
        return total

    c2.wait_recv()
    add_own(b2c, ut2)
    x2s = [send(b2c.at[xs(a)], b2x.at[a - 1], device(xs(a), y, z, c)) for a in range(1, NX)]
    c1.wait_recv()
    add_own(b1c, ut1)
    x1s = [send(b1c.at[pl.ds(xs(a) * 2, 2)], b1x.at[a - 1], device(xs(a), y, z, c)) for a in range(1, NX)]
    c0.wait_recv()
    add_own(b0c, ut0)
    y0s = [send(b0c.at[pl.ds(ys(b) * NX, NX)], b0y.at[b - 1], device(x, ys(b), z, c)) for b in range(1, NY)]

    arrive(x2s)
    b2s[...] = b2c[x] + b2x[0] + b2x[1] + b2x[2]
    z2s = z_stage(b2s, b2z)
    arrive(x1s)
    for i in range(2):
        b1s[i] = b1c[x * 2 + i] + b1x[0, i] + b1x[1, i] + b1x[2, i]
    y1s = send(b1s.at[1 - yy], b1y, device(x, partner, z, c))

    r2 = z_sum(b2s, b2z, z2s)
    g2[x] = r2
    a2 = [send(g2.at[x], g2.at[x], device(xs(a), y, z, c)) for a in range(1, NX)]
    y1s.wait_recv()
    b1t[...] = b1s[yy] + b1y[...]
    z1s = z_stage(b1t, b1z)
    arrive(y0s)
    for i in range(NX):
        b0s[i] = b0c[y * NX + i] + b0y[0, i] + b0y[1, i] + b0y[2, i]
    x0s = [send(b0s.at[xs(a)], b0x.at[a - 1], device(xs(a), y, z, c)) for a in range(1, NX)]

    def joined(ref):
        return jnp.concatenate([ref[i] for i in range(ref.shape[0])], axis=1)

    def spill(value, ref):
        for i in range(ref.shape[0]):
            ref[i] = value[:, i * LANES : (i + 1) * LANES]

    def columns(start, size):
        return m_ref[:, start : start + size]

    here1 = yy * NX + x
    here0 = y * NX + x

    def scatter_half(part, landed):
        return [
            send(part.at[(yy if b == 0 else 1 - yy) * NX + xs(a)], landed.at[k], device(xs(a), pair_y(b), z, c))
            for k, (a, b) in enumerate(half)
        ]

    def gather_half(whole):
        return [send(whole.at[here1], whole.at[here1], device(xs(a), pair_y(b), z, c)) for a, b in half]

    def scatter_plane(part, landed):
        return [
            send(part.at[ys(b) * NX + xs(a)], landed.at[k], device(xs(a), ys(b), z, c))
            for k, (a, b) in enumerate(plane)
        ]

    def gather_plane(whole):
        return [send(whole.at[here0], whole.at[here0], device(xs(a), ys(b), z, c)) for a, b in plane]

    def summed(part, here, landed, batch):
        arrive(batch)
        total = part[here]
        for k in range(landed.shape[0]):
            total = total + landed[k]
        return total

    s0_scale, s1_scale = weight_scale(0), weight_scale(1)

    arrive(a2)
    solved2 = small_dot(joined(g2), columns(G2, 512), NT)
    spill(small_dot(solved2, columns(E21, 1024), NN), p1)
    batch = scatter_half(p1, p1r)
    r1 = z_sum(b1t, b1z, z1s)
    arrive(x0s)
    b0t[...] = b0s[x] + b0x[0] + b0x[1] + b0x[2]
    z0s = z_stage(b0t, b0z)
    g1[here1] = r1 - s1_scale * summed(p1, here1, p1r, batch)
    batch = gather_half(g1)
    up0 = small_dot(solved2, columns(E20, 2048), NN)
    arrive(batch)
    solved1 = small_dot(joined(g1), columns(G1, 1024), NT)
    spill(up0 + small_dot(solved1, columns(E10, 2048), NN), p0)
    batch = scatter_plane(p0, p0r)
    r0 = z_sum(b0t, b0z, z0s)
    g0[here0] = r0 - s0_scale * summed(p0, here0, p0r, batch)
    arrive(gather_plane(g0))
    solved0 = small_dot(joined(g0), columns(G0, 2048), NT)

    def hand_out(whole, result):
        result[:, spread, :] = whole[...]
        return [send(whole, result.at[:, spread, :], device(x, y, zs(d), c)) for d in range(1, NZ)]

    spill(small_dot(solved0, columns(G0, 2048), NN), q0)
    batch = scatter_plane(q0, q0r)
    h0[here0] = summed(q0, here0, q0r, batch)
    arrive(gather_plane(h0))
    d0s = hand_out(h0, x0)
    found0 = joined(h0)
    y1 = solved1 - s0_scale * small_dot(found0, columns(E10, 2048), NT)
    spill(small_dot(y1, columns(G1, 1024), NN), q1)
    batch = scatter_half(q1, q1r)
    y2 = solved2 - s0_scale * small_dot(found0, columns(E20, 2048), NT)
    h1[here1] = summed(q1, here1, q1r, batch)
    arrive(gather_half(h1))
    d1s = hand_out(h1, x1)
    y2 = y2 - s1_scale * small_dot(joined(h1), columns(E21, 1024), NT)
    spill(small_dot(y2, columns(G2, 512), NN), q2)
    batch = [send(q2.at[xs(a)], q2r.at[a - 1], device(xs(a), y, z, c)) for a in range(1, NX)]
    h2[x] = summed(q2, x, q2r, batch)
    arrive([send(h2.at[x], h2.at[x], device(xs(a), y, z, c)) for a in range(1, NX)])
    d2s = hand_out(h2, x2)
    last = []
    for result, batch in ((x0, d0s), (x1, d1s), (x2, d2s)):
        arrive(batch)
        last.append(send(result.at[:, mine, :], result.at[:, mine, :], sibling))
    arrive(last)
    for copy in copies:
        copy.wait_send()


N_COPIES = 3 + 3 + 3 + 3 + 7 + 1 + 3 + 7 + 3 + 7 + 7 + 7 + 15 + 15 + 15 + 15 + 7 + 7 + 7 + 7 + 3 + 3 + 7 + 3


def chain(ut0, ut1, ut2, matrix):
    def piece(*lead, rows=COLS):
        return pltpu.VMEM((*lead, rows, LANES), F32)

    scratch = [
        piece(4, rows=LANES), piece(8, rows=LANES), piece(16, rows=LANES),
        piece(3, rows=LANES), piece(rows=LANES), piece(7),
        piece(3, 2, rows=LANES), piece(2, rows=LANES), piece(rows=LANES), piece(rows=LANES), piece(7),
        piece(3, 4, rows=LANES), piece(4, rows=LANES), piece(3, rows=LANES), piece(rows=LANES), piece(7),
        piece(4), piece(8), piece(7), piece(8), piece(16), piece(15), piece(16),
        piece(16), piece(15), piece(16), piece(8), piece(7), piece(8), piece(4), piece(3), piece(4),
        pltpu.SemaphoreType.DMA((N_COPIES,)), pltpu.SemaphoreType.DMA((N_COPIES,)),
    ]
    vmem = pl.BlockSpec(memory_space=pltpu.VMEM)
    return pl.pallas_call(
        chain_kernel,
        out_shape=[jax.ShapeDtypeStruct((n, RHS, LANES), F32) for n in (16, 8, 4)],
        in_specs=[vmem] * 4,
        out_specs=[vmem] * 3,
        scratch_shapes=scratch,
        compiler_params=pltpu.CompilerParams(
            collective_id=0, has_side_effects=True, vmem_limit_bytes=48 * 1024 * 1024
        ),
    )(ut0, ut1, ut2, matrix)


def rounded(value):
    return lax.reduce_precision(value, 8, 7)


def parts(value):
    high = rounded(value)
    return high.astype(BF16), rounded(value - high).astype(BF16)


def fast_dot(left, right, dims):
    lh, ll = parts(left)
    rh, rl = parts(right)
    dot = functools.partial(lax.dot_general, dimension_numbers=dims, preferred_element_type=F32)
    return dot(lh, rh) + (dot(lh, rl) + dot(ll, rh))


def exact_right_dot(left, right, dims):
    lh, ll = parts(left)
    dot = functools.partial(lax.dot_general, dimension_numbers=dims, preferred_element_type=F32)
    return dot(lh, right) + dot(ll, right)


def triangle(strict, diagonal):
    order_size = strict.shape[-1]
    return jnp.tril(strict, -1) + diagonal[..., :, None] * jnp.eye(order_size, dtype=F32)


def solve_lower(matrix, right_side, transposed):
    return lax.linalg.triangular_solve(matrix, right_side, left_side=True, lower=True, transpose_a=transposed)


def reorder(rows):
    return rows // 512 * 512 + rows // 16 % 4 * 128 + rows // 64 % 8 * 16 + rows % 16


def reorder_columns(value):
    lead, width = value.shape
    value = value.reshape(lead, width // 512, NZ, NX, 16)
    return jnp.swapaxes(value, 2, 3).reshape(lead, width)


def body(rhs_sub, rhs_sep, sub_factor, sub_diag, sep_factor, sep_diag, sub_update, update_rows, sep_update):
    position = lax.axis_index(("leaf", "panel"))
    inverses = []
    for level in range(LEVELS):
        node_rows = ROWS >> level
        start = sum(ROWS >> k for k in range(level))
        own = position % (256 >> level) * BLK
        strict = sep_factor[:, start : start + node_rows]
        row_ids = own + lax.broadcasted_iota(jnp.int32, (BLK, node_rows), 0)
        col_ids = lax.broadcasted_iota(jnp.int32, (BLK, node_rows), 1)
        lower = jnp.where(col_ids < row_ids, strict, 0.0)
        inverses.append(lower + jnp.where(col_ids == row_ids, sep_diag[level][:, None], 0.0))
    turned = sep_update[0].T
    e10, e20, e21 = turned[:, :2048], turned[:, 2048:4096], turned[:, 4096:]
    matrix = reorder_columns(jnp.concatenate([inverses[2], e21, inverses[1], e20, e10, inverses[0]], axis=1))
    pairs = [[2 * k, 2 * k + 1] for k in range(NX)]
    lines = [[k * NZ + j for j in range(NZ)] for k in range(NY)]
    matrix = lax.all_gather(matrix, "panel", axis=0, tiled=True, axis_index_groups=pairs)
    matrix = lax.all_gather(matrix, "leaf", axis=0, tiled=True, axis_index_groups=lines)

    sub_lower = triangle(sub_factor[0], sub_diag[0])
    sub_solved = solve_lower(sub_lower, rhs_sub[0], False)
    coupling = sub_update[0]
    terms = fast_dot(sub_solved, coupling, (((0,), (1,)), ((), ())))
    sums, picks = [], []
    start = 0
    for level in range(LEVELS):
        node_rows = ROWS >> level
        count = node_rows // 2
        rows = reorder(update_rows[0, start : start + count])
        ids = lax.broadcasted_iota(jnp.int32, (count, node_rows), 1)
        pick = (rows[:, None] == ids).astype(BF16)
        own = position % (256 >> level) * BLK + jnp.arange(BLK, dtype=jnp.int32)
        mark = (reorder(own)[:, None] == lax.broadcasted_iota(jnp.int32, (BLK, node_rows), 1)).astype(F32)
        placed = jnp.dot(rhs_sep[level].T, mark, precision=lax.Precision.HIGHEST)
        sums.append(placed - weight_scale(level) * exact_right_dot(terms[:, start : start + count], pick, NN))
        picks.append(pick)
        start += count
    ut0 = sums[0].reshape(RHS, 16, LANES).swapaxes(0, 1)
    ut1 = sums[1].reshape(RHS, 2, NX, LANES).transpose(2, 1, 0, 3).reshape(8, RHS, LANES)
    ut2 = sums[2].reshape(RHS, NX, LANES).swapaxes(0, 1)
    found = chain(ut0, ut1, ut2, matrix)

    current = sub_solved
    own_results = []
    start = 0
    for level in range(LEVELS):
        node_rows = ROWS >> level
        count = node_rows // 2
        whole = found[level].swapaxes(0, 1).reshape(RHS, node_rows)
        picked = exact_right_dot(whole, picks[level], NT)
        current = current - weight_scale(level) * fast_dot(coupling[start : start + count], picked, (((0,), (1,)), ((), ())))
        own = position % (256 >> level) * BLK
        at = reorder(own)
        block = lax.dynamic_index_in_dim(found[level], at // LANES, 0, keepdims=False)
        own_results.append(lax.dynamic_slice_in_dim(block, at % LANES, BLK, 1).T)
        start += count
    result_sub = solve_lower(sub_lower, current, True)
    return result_sub[None], jnp.stack(own_results)


def solution(mesh):
    both = ("leaf", "panel")
    in_specs = (
        P(both, None, None), P(None, both, None), P(both, None, None), P(both, None), P(both, None),
        P(None, both), P(both, None, None), P(both, None), P(both, None, None),
    )
    out_specs = (P(both, None, None), P(None, both, None))
    return jax.shard_map(body, mesh=mesh, in_specs=in_specs, out_specs=out_specs, check_vma=False)
```

time: 759 us -> 252 us (0.33)
  waiting for transfers between devices: 417 us -> 0.02 us
  starting transfers between devices: 125 us -> 0.04 us
  Pallas kernels: 0 us -> 105 us
  blocking collectives: 44 us -> 5.19 us
  other arithmetic: 73.7 us -> 48.7 us
  matrix products: 53.3 us -> 40 us
  local copies, waits for them, and re-layouts: 20.6 us -> 32.1 us
    reduce_scatter x6 -> x0, waiting for transfers between devices: 195 us -> none  [sectioned_sum(): lax.psum_scatter(partial_value, 'panel', scatter_dimension=0, tiled=True)]
    all_gather x4 -> x1, waiting for transfers between devices: 147 us -> 0.01 us  [body(): lax.all_gather(matrix, 'leaf', axis=0, tiled=True, axis_index_groups=lines)]
    ppermute x48 -> x0, starting transfers between devices: 124 us -> none  [swapped(): lax.ppermute(shard, axis, [(i, i ^ 1 << bit) for i in range(lax.axis_size...]
    pallas_call x0 -> x1, Pallas kernels: none -> 105 us  [chain(): pl.pallas_call(chain_kernel, out_shape=[jax.ShapeDtypeStruct((n, RHS, LAN...]
    ppermute x48 -> x0, waiting for transfers between devices: 74.6 us -> none  [swapped(): lax.ppermute(shard, axis, [(i, i ^ 1 << bit) for i in range(lax.axis_size...]
    all_gather x2 -> x1, blocking collectives: 44 us -> 5.19 us  [body(): lax.all_gather(matrix, 'panel', axis=0, tiled=True, axis_index_groups=pairs)]
    dot_general x18 -> x27, matrix products: 46.2 us -> 32.9 us  [the longest x12 17.4 us: exact_right_dot(): return dot(lh, right) + dot(ll, right)]
    scatter-add x3 -> x0, other arithmetic: 12.7 us -> none  [body(): partial_value = jnp.zeros((node_rows, columns), jnp.float32).at[rows_used...]
  transfers between devices with their start and end apart: 58 -> 1, of which waited for: 55 -> 0; matrix products, arithmetic and copies ran while one was open for 3% -> 29% of each run, Pallas kernels for 0% -> 0%
where the time goes in v1:
time: 252 us; the launch traced here: 247 us
  Pallas kernels  105 us (42%)
  other arithmetic  48.7 us (19%)
  matrix products  40 us (16%)
  local copies, waits for them, and re-layouts  32.1 us (13%)
  between operations  15.3 us (6%)
  blocking collectives  5.19 us (2%)
    pallas_call x1, Pallas kernels, chain(): pl.pallas_call(chain_kernel, out_shape=[jax.ShapeDtypeStruct((n, RHS, LAN...  105 us
    another operation x3, other arithmetic, solve_lower(): lax.linalg.triangular_solve(matrix, right_side, left_side=True, lower=Tru...  39.5 us
    dot_general x12, matrix products, exact_right_dot(): return dot(lh, right) + dot(ll, right)  17.4 us
    dot_general x12, matrix products, fast_dot(): return dot(lh, rh) + (dot(lh, rl) + dot(ll, rh))  12.6 us
    another operation x12, local copies, waits for them, and re-layouts  7.83 us
    another operation x14, matrix products, solve_lower(): lax.linalg.triangular_solve(matrix, right_side, left_side=True, lower=Tru...  7.08 us
    unnamed x53, local copies, waits for them, and re-layouts  6.76 us
    transpose x3, local copies, waits for them, and re-layouts, body(): whole = found[level].swapaxes(0, 1).reshape(RHS, node_rows)  5.4 us
  transfers between devices with their start and end apart: 1, of which 0 were waited for; matrix products, arithmetic and copies ran while one was open for 29% of the time, Pallas kernels for 0%

profile of v1, /device:TPU:1, one launch (start us, length us, event | category | flops | bytes accessed | tf_op | source)
XLA Modules:
  0.0 247.1 jit_solution(16393077743057154262)
XLA Ops:
  7.2 0.5 fusion.164
  7.8 0.8 slice_bitcast_fusion.12
  8.6 0.8 add_dynamic-update-slice_fusion.2
  9.4 0.8 slice_dynamic-update-slice_fusion.2
  10.1 0.8 add_dynamic-update-slice_fusion.1
  11.0 0.8 slice_dynamic-update-slice_fusion.1
  11.8 0.8 slice_dynamic-update-slice_fusion
  12.7 0.9 add_dynamic-update-slice_fusion
  13.6 1.6 reshape.587
  15.2 1.6 copy.34
  16.8 3.3 %reshape.588 = f32[8,8704]{1,0:T(8,128)S(1)} reshape(f32[8,17,4,8,16]{4,3,2,1,0:T(8,128)} %copy.34) | data formatting | bytes 557056 | tf_op jit(solution)/shard_map/reshape | solution.py:319
  20.1 5.2 %all_gather.6 = f32[16,8704]{1,0:T(8,128)} all-gather(f32[8,8704]{1,0:T(8,128)S(1)} %reshape.588), channel_id=1, replica_groups={{0,1},{2,3},{4,5},{6,7},{8,9},{10,11},{12,13},{14,15},{16,17},{18,19},{..., dimensions={0}, use_global_device_ids=true | all-gather | bytes 835584 | tf_op jit(solution)/shard_map/all_gather | solution.py:339
  26.0 8.4 %while.1 = (s32[]{:T(128)}, f32[512,512]{1,0:T(8,128)S(1)}, s32[4,2]{0,1:T(2,128)S(1)}, f32[4,128,128]{2,1,0:T(8,128)S(1)}, s32[]{:T(128)}) while((s32[]{:T(128)}, f32[512,512]{1,0:T(8,128)S(1)}, s32[4,2]{0,1:T(2,128)S(1)}, f32[4,128,128]{2,1,0:T(8,128)S(1)}, s32[]{:T(128)}) %tuple.30), condition=%wide.while_cond, body=%wide.while_body.sunk | while | flops 2 | bytes 131189 | solution.py:309
  26.5 0.6 fusion.203
  27.1 1.3 bitcast_dynamic-update-slice_fusion.2
  28.5 0.6 fusion.203
  29.1 1.3 bitcast_dynamic-update-slice_fusion.2
  30.5 0.6 fusion.203
  31.0 1.3 bitcast_dynamic-update-slice_fusion.2
  32.5 0.6 fusion.203
  33.0 1.3 bitcast_dynamic-update-slice_fusion.2
  34.4 39.3 %custom-call.5 = f32[4,128,128]{1,2,0:T(8,128)S(1)} custom-call(f32[4,128,128]{2,1,0:T(8,128)S(1)} %get-tuple-element.15), custom_call_target="InvertDiagBlocksLowerTriangular" | custom-call | tf_op jit(solution)/shard_map/triangular_solve | solution.py:309
  75.3 0.4 convolution_subtract_fusion.2
  76.0 2.9 %fusion.57 = f32[256,1792]{1,0:T(8,128)S(1)} fusion(f32[1,1792,512]{2,1,0:T(8,128)} %param.15, f32[128,256]{1,0:T(8,128)S(1)} %fusion.121, f32[128,256]{1,0:T(8,128)S(1)} %fusion.120, f32[128,256]{1,0:T(8,128)S(1)} %fusion.118, f32[128,256]{1,0:T(8,128)S(1)} %fusion.111), kind=kOutput, calls=%fused_computation.106 | convolution fusion | flops 472252416 | bytes 6029312 | tf_op jit(solution)/shard_map/dot_general | solution.py:294
  79.3 0.7 fusion.22
  80.1 0.7 fusion.10
  80.8 2.5 %fusion.2 = f32[256,2048]{0,1:T(8,128)S(1)} fusion(s32[1024]{0:T(1024)S(1)} %fusion.135, f32[256,1792]{1,0:T(8,128)S(1)} %fusion.10), kind=kOutput, calls=%fused_computation.5 | convolution fusion | flops 1076887552 | bytes 3149824 | tf_op jit(solution)/shard_map/dot_general | solution.py:300
  83.4 2.5 %fusion.13 = f32[256,2048]{0,1:T(8,128)S(1)} fusion(f32[256,2048]{0,1:T(8,128)S(1)} %fusion.2, s32[1024]{0:T(1024)S(1)} %fusion.135, f32[256,1792]{1,0:T(8,128)S(1)} %fusion.10), kind=kOutput, calls=%fused_computation.24 | convolution fusion | flops 1077411840 | bytes 5246976 | tf_op jit(solution)/shard_map/dot_general | solution.py:300
  85.9 1.1 fusion.11
  87.0 2.0 copy.27
  89.1 1.9 fusion.20
  90.9 1.9 fusion.26
  92.8 0.7 fusion.24
  93.9 1.4 fusion.73
  95.3 1.4 fusion.35
  96.7 1.2 fusion.28
  97.9 1.0 copy.33
  98.9 1.0 copy-done
  99.9 105.2 %shard_map.104 = (f32[16,256,128]{2,1,0:T(8,128)S(1)}, f32[8,256,128]{2,1,0:T(8,128)S(1)}, f32[4,256,128]{2,1,0:T(8,128)S(1)}) custom-call(f32[16,256,128]{2,1,0:T(8,128)} %bitcast.188, f32[8,256,128]{2,1,0:T(8,128)S(1)} %bitcast.181, f32[4,256,128]{2,1,0:T(8,128)S(1)} %bitcast.183, f32[128,8704]{1,0:T(8,128)} %all-gather.2.cloned.1.call-done.m_ref), custom_call_target="tpu_custom_call" | custom-call | tf_op jit(solution)/shard_map/pallas_call | solution.py:269
  205.1 1.0 copy-done.1
  206.1 0.8 copy-done.3
  206.9 2.0 copy.35
  208.9 1.9 reduce-precision_convert_fusion.2
  210.8 1.9 fusion
  212.7 1.9 fusion.27
  214.8 1.3 convolution_bitcast_fusion.8
  216.1 1.3 convolution_bitcast_fusion.7
  217.5 1.3 copy.38
  218.8 1.4 reduce-precision_convert_fusion.4
  220.2 0.7 fusion.18
  220.9 0.7 fusion.34
  221.5 0.6 copy-done.6
  222.2 0.4 fusion.68
  222.6 1.2 fusion.39
  223.7 2.0 copy.41
  225.8 1.3 fusion.65
  227.8 1.4 fusion.88
  229.6 1.6 fusion.41
  232.5 1.1 convolution_subtract_fusion.4
  233.9 1.3 convolution_subtract_fusion.1
  235.5 1.4 convolution_subtract_fusion
  237.2 0.8 maximum_bitcast_fusion
  238.0 1.0 constant_dynamic-slice_fusion.1
  239.4 0.6 pad_maximum_fusion.1
  (91 shorter events, 6.7 us)
Async XLA Ops:
  7.2 91.7 %all-gather.2.cloned.1.call-start = ((), (), s32[]{:S(2)}) async-start(), calls=%async_computation | async-start | bytes 5013504 | tf_op jit(solution)/shard_map/all_gather | solution.py:340
  16.8 9.0 %copy-start.20 = (f32[1,512,512]{2,1,0:T(8,128)S(1)}, f32[1,512,512]{2,1,0:T(8,128)}, u32[]{:S(2)}) copy-start(f32[1,512,512]{2,1,0:T(8,128)} %param.11) | copy-start | bytes 3145732
  16.8 9.0 %copy-start.23 = (f32[1,512]{1,0:T(1,128)S(1)}, f32[1,512]{1,0:T(1,128)}, u32[]{:S(2)}) copy-start(f32[1,512]{1,0:T(1,128)} %param.12) | copy-start | bytes 6148
  25.3 48.4 %slice-start = ((s32[1,1792]{1,0:T(1,128)}), s32[1,1024]{1,0:T(1,128)S(1)}, s32[]{:S(2)}) async-start(s32[1,1792]{1,0:T(1,128)} %param.16), calls=%async_computation.1 | async-start | bytes 8192 | tf_op jit(solution)/shard_map/slice | solution.py:351
  25.3 48.5 %copy-start.21 = (f32[1,512,256]{2,1,0:T(8,128)S(1)}, f32[1,512,256]{2,1,0:T(8,128)}, u32[]{:S(2)}) copy-start(f32[1,512,256]{2,1,0:T(8,128)} %param.9) | copy-start | bytes 1572868
  34.4 44.6 %copy-start.13 = (f32[512,512]{1,0:T(8,128)}, f32[512,512]{1,0:T(8,128)S(1)}, u32[]{:S(2)}) copy-start(f32[512,512]{1,0:T(8,128)S(1)} %get-tuple-element.84) | copy-start | bytes 3145732
  73.7 5.3 %copy-start.18 = (f32[4,128,128]{1,2,0:T(8,128)}, f32[4,128,128]{1,2,0:T(8,128)S(1)}, u32[]{:S(2)}) copy-start(f32[4,128,128]{1,2,0:T(8,128)S(1)} %custom-call.5) | copy-start | bytes 786436
  76.0 4.0 %copy-start.14 = (f32[128,256]{1,0:T(8,128)}, f32[128,256]{1,0:T(8,128)S(1)}, u32[]{:S(2)}) copy-start(f32[128,256]{1,0:T(8,128)S(1)} %fusion.121) | copy-start | bytes 393220
  76.0 3.3 %copy-start.4 = (f32[1,1792,512]{2,1,0:T(8,128)S(1)}, f32[1,1792,512]{2,1,0:T(8,128)}, u32[]{:S(2)}) copy-start(f32[1,1792,512]{2,1,0:T(8,128)} %param.15) | copy-start | bytes 11010052
  80.8 2.5 %copy-start.12 = (f32[256,1792]{1,0:T(8,128)}, f32[256,1792]{1,0:T(8,128)S(1)}, u32[]{:S(2)}) copy-start(f32[256,1792]{1,0:T(8,128)S(1)} %fusion.10) | copy-start | bytes 5505028
  83.3 2.5 %copy-start.22 = (f32[3,8,256]{2,1,0:T(8,128)S(1)}, f32[3,8,256]{2,1,0:T(8,128)}, u32[]{:S(2)}) copy-start(f32[3,8,256]{2,1,0:T(8,128)} %param.10) | copy-start | bytes 73732
  87.0 2.0 slice-start.1
  92.8 1.1 slice-start.2
  93.9 2.8 %copy-start.24 = (s32[8]{0:T(128)S(1)}, s32[8]{0:T(128)}, u32[]{:S(2)}) copy-start(s32[8]{0:T(128)} %get-tuple-element.37) | copy-start | bytes 100
  98.9 1.0 copy-start
  205.1 1.0 copy-start.1
  206.1 0.8 copy-start.3
  212.7 2.0 copy-start.5
  214.8 2.7 %copy-start.8 = (f32[256,1024]{1,0:T(8,128)}, f32[256,1024]{1,0:T(8,128)S(1)}, u32[]{:S(2)}) copy-start(f32[256,1024]{1,0:T(8,128)S(1)} %fusion.27) | copy-start | bytes 3145732
  216.1 1.4 copy-start.2
  220.2 2.0 copy-start.6
  222.2 1.5 copy-start.10
  225.8 3.5 %copy-start.7 = (f32[1,1792,512]{2,1,0:T(8,128)S(1)}, f32[1,1792,512]{2,1,0:T(8,128)}, u32[]{:S(2)}) copy-start(f32[1,1792,512]{2,1,0:T(8,128)} %param.15) | copy-start | bytes 11010052
  227.4 2.1 copy-start.9
  227.4 2.1 copy-start.15
  227.4 2.1 copy-start.16
  229.6 1.7 copy-start.11
  229.6 1.7 copy-start.17
  231.2 1.0 copy-start.19
Sparse Core Ops, SparseCore 0:
  25.5 58.2 all-gather.1

commit v2 on v1

v2 whole, which is shorter than its diff:
```python
import jax
import jax.numpy as jnp
from jax import lax
from jax.experimental import pallas as pl
from jax.experimental.pallas import tpu as pltpu
from jax.sharding import PartitionSpec as P

MESH = pl.DeviceIdType.MESH
F32 = jnp.float32
BF16 = jnp.bfloat16
NN = (((1,), (0,)), ((), ()))
NT = (((1,), (1,)), ((), ()))
TN = (((0,), (0,)), ((), ()))

NX, NY, NZ = 4, 4, 8
ROWS, RHS, LOC, BLK = 2048, 256, 512, 8
LEVELS = 3
LANES = 128
COLS = 16
G2, E21, G1, E20, E10, G0, WIDE = 0, 512, 1536, 2560, 4608, 6656, 8704


def weight_scale(target):
    fan_total = (256 >> target) * LOC // 2 + (LEVELS - 1 - target) * (ROWS >> target)
    return float(fan_total) ** (-0.5)


def split(value):
    high = value.astype(BF16)
    return high, (value - high.astype(F32)).astype(BF16)


def small_dot(left, right, dims):
    left_high, left_low = split(left)
    right_high, right_low = split(right)
    rows = left.shape[0]
    both = jnp.concatenate([left_high, left_low], axis=0)
    first = lax.dot_general(both, right_high, dims, preferred_element_type=F32)
    second = lax.dot_general(left_high, right_low, dims, preferred_element_type=F32)
    return first[:rows] + first[rows:] + second


def place():
    leaf, panel = lax.axis_index("leaf"), lax.axis_index("panel")
    return panel // 2, leaf // NZ, leaf % NZ, panel % 2


def device(x, y, z, c):
    return (y * NZ + z, x * 2 + c)


def split3(value):
    high = value.astype(BF16)
    rest = value - high.astype(F32)
    middle = rest.astype(BF16)
    return high, middle, (rest - middle.astype(F32)).astype(BF16)


def exact_dot(left, right):
    return jnp.dot(left, right, precision=lax.Precision.HIGHEST, preferred_element_type=F32)


def iota(shape, dim):
    return lax.broadcasted_iota(jnp.int32, shape, dim)


def reorder(rows):
    return (rows >> 9 << 9) + ((rows >> 4 & 3) << 7) + ((rows >> 6 & 7) << 4) + (rows & 15)


def sub_start(level):
    return sum(ROWS >> k + 1 for k in range(level))


def row_start(level):
    return sum(ROWS >> k for k in range(level))


def invert(factor, scale, inverse):
    lane = iota((32, LANES), 1)
    row, col = iota((LANES, LANES), 0), iota((LANES, LANES), 1)
    blocks, packed = [], []
    for g in range(4):
        at = slice(g * LANES, (g + 1) * LANES)
        block = jnp.where(row > col, factor[at, at] * scale[:, at], 0.0)
        blocks.append(block)
        parts = [jnp.where(lane >> 5 == q, block[32 * q : 32 * q + 32], 0.0) for q in range(4)]
        packed.append(parts[0] + parts[1] + parts[2] + parts[3])
    unit = (iota((32, LANES), 0) == (lane & 31)).astype(F32)
    found = [unit] * 4
    for k in range(31):
        index = (lane & 96) + k
        for g in range(4):
            coefficient = jnp.take_along_axis(packed[g], index, axis=1, mode="promise_in_bounds")
            found[g] = found[g] - coefficient * found[g][k : k + 1, :]
    whole = []
    for g in range(4):
        total = jnp.concatenate([jnp.where(lane >> 5 == q, found[g], 0.0) for q in range(4)], axis=0)
        whole.append(total)
    for bit in (5, 6):
        below = (row >> bit + 1 == col >> bit + 1) & (row >> bit > col >> bit)
        inner = [exact_dot(jnp.where(below, blocks[g], 0.0), whole[g]) for g in range(4)]
        whole = [whole[g] - exact_dot(whole[g], inner[g]) for g in range(4)]
    inverse[...] = jnp.zeros_like(inverse)
    for h in range(2):
        first = slice(h * 256, h * 256 + 128)
        second = slice(h * 256 + 128, h * 256 + 256)
        inner = exact_dot(factor[second, first] * scale[:, first], whole[2 * h])
        inverse[first, first] = whole[2 * h]
        inverse[second, second] = whole[2 * h + 1]
        inverse[second, first] = -exact_dot(whole[2 * h + 1], inner)
    inner = exact_dot(factor[256:, :256] * scale[:, :256], inverse[:256, :256])
    inverse[256:, :256] = -exact_dot(inverse[256:, 256:], inner)


def separator_rows(sep_factor, sep_diag, turned, position):
    inverses = []
    eye = iota((BLK, BLK), 0) == iota((BLK, BLK), 1)
    for level in range(LEVELS):
        node_rows = ROWS >> level
        start = row_start(level)
        strict = sep_factor[:, start : start + node_rows]
        diagonal = jnp.sum(jnp.where(eye, sep_diag[level : level + 1, :], 0.0), axis=1, keepdims=True)
        own = position % (256 >> level) * BLK + iota((BLK, node_rows), 0)
        cols = iota((BLK, node_rows), 1)
        inverses.append(jnp.where(cols < own, strict, 0.0) + jnp.where(cols == own, diagonal, 0.0))
    e10, e20, e21 = turned[:, :2048], turned[:, 2048:4096], turned[:, 4096:]
    pieces = [inverses[2], e21, inverses[1], e20, e10, inverses[0]]
    blocks = [piece[:, i : i + 512] for piece in pieces for i in range(0, piece.shape[1], 512)]
    stacked = jnp.concatenate(blocks, axis=0)
    swap = jnp.where(reorder(iota((512, 512), 0)) == iota((512, 512), 1), 1.0, 0.0).astype(BF16)
    high, middle, low = split3(stacked)
    return (
        jnp.dot(high, swap, preferred_element_type=F32)
        + jnp.dot(middle, swap, preferred_element_type=F32)
        + jnp.dot(low, swap, preferred_element_type=F32)
    )


def whole_kernel(
    diag, rows, rhs_sep, sep_factor, sep_diag, turned, factor_hbm, rhs_hbm, update_hbm,
    out_sub, out_sep,
    factor, rhs, update, inverse, solved_t, current, terms, update_high, update_low, moved_high, moved_low,
    ut0, ut1, ut2, m_ref, x0, x1, x2,
    b2c, b1c, b0c, b2x, b2s, b2z, b1x, b1s, b1y, b1t, b1z, b0y, b0s, b0x, b0t, b0z,
    g2, p1, p1r, g1, p0, p0r, g0, q0, q0r, h0, q1, q1r, h1, q2, q2r, h2,
    lsem, ssem, rsem,
):
    x, y, z, c = place()
    position = lax.axis_index("leaf") * 8 + lax.axis_index("panel")
    partner = y + 1 - 2 * (y % 2)
    yy = y % 2
    sibling = device(x, y, z, 1 - c)
    plane = [(a, b) for a in range(NX) for b in range(NY)][1:]
    half = [(a, b) for a in range(NX) for b in range(2)][1:]

    loads = [
        pltpu.make_async_copy(src, dst, lsem.at[i])
        for i, (src, dst) in enumerate(((factor_hbm, factor), (rhs_hbm, rhs), (update_hbm, update)))
    ]
    for load in loads:
        load.start()

    def xs(a):
        return (x + a) % NX

    def ys(b):
        return (y + b) % NY

    def zs(d):
        return (z + d) % NZ

    def pair_y(b):
        return partner if b else y

    barrier = pltpu.get_barrier_semaphore()
    greeted = [device(xs(a), ys(b), z, c) for a, b in plane]
    greeted += [device(x, y, zs(d), c) for d in range(1, NZ)] + [sibling]
    for peer in greeted:
        pl.semaphore_signal(barrier, inc=1, device_id=peer, device_id_type=MESH)

    copies = []

    def send(src, dst, peer):
        at = len(copies)
        copy = pltpu.make_async_remote_copy(
            src_ref=src, dst_ref=dst, send_sem=ssem.at[at], recv_sem=rsem.at[at],
            device_id=peer, device_id_type=MESH,
        )
        copy.start()
        copies.append(copy)
        return copy

    def arrive(batch):
        for copy in batch:
            copy.wait_recv()

    own_rows = separator_rows(sep_factor, sep_diag, turned, position)
    for i in range(WIDE // 512):
        m_ref[z, c, :, i * 512 : (i + 1) * 512] = own_rows[i * BLK : (i + 1) * BLK]
    pl.semaphore_wait(barrier, len(greeted))

    def pass_on(block, columns, peer):
        ref = m_ref.at[block, c, :, columns]
        return send(ref, ref, peer)

    everything, front, back = pl.ds(0, WIDE), pl.ds(0, WIDE // 2), pl.ds(WIDE // 2, WIDE // 2)
    right, left = device(x, y, zs(1), c), device(x, y, zs(NZ - 1), c)
    ring = [[pass_on(z, everything, right), pass_on(z, everything, left)]]
    shared = [pass_on(z, everything, sibling)]

    def ring_step():
        step = len(ring)
        arrive(ring[-1])
        from_left, from_right = zs(NZ - step), zs(step)
        if step < 3:
            ring.append([pass_on(from_left, everything, right), pass_on(from_right, everything, left)])
        elif step == 3:
            ring.append([pass_on(from_left, front, right), pass_on(from_right, back, left)])
        else:
            ring.append([])
        if step < 4:
            shared.append(pass_on(from_left, everything, sibling))
            shared.append(pass_on(from_right, everything, sibling))
        else:
            shared.append(pass_on(from_left, everything, sibling))

    scale = 1.0 / diag[...]
    loads[0].wait()
    invert(factor, scale, inverse)
    loads[1].wait()
    right_t = rhs[...].T
    solved_t[...] = small_dot(right_t, inverse[...], NT) * scale
    current[...] = solved_t[...]
    ring_step()
    loads[2].wait()
    solved_high, solved_low = split(solved_t[...])
    solved_both = jnp.concatenate([solved_high, solved_low], axis=0)

    def coupling_terms(level):
        def step(i, carry):
            at = pl.ds(pl.multiple_of(sub_start(level) + i * 256, 256), 256)
            high, low = split(update[at, :])
            update_high[at, :] = high
            update_low[at, :] = low
            first = lax.dot_general(solved_both, high, NT, preferred_element_type=F32)
            second = lax.dot_general(solved_high, low, NT, preferred_element_type=F32)
            top, bottom = split(first[:RHS] + first[RHS:] + second)
            terms[:RHS, at] = top
            terms[RHS:, at] = bottom
            return carry

        lax.fori_loop(0, (ROWS >> level) // 512, step, 0)

    places = []
    for level in range(LEVELS):
        count = ROWS >> level + 1
        places.append(reorder(rows[:, sub_start(level) : sub_start(level) + count]))

    def chosen(level, i):
        count = ROWS >> level + 1
        ids = iota((256, count), 0) + i * 256
        return jnp.where(ids == places[level], 1.0, 0.0).astype(BF16)

    own_chunk = [y * NX + x, x * 2 + yy, x]
    mark = jnp.where(iota((BLK, LANES), 1) == z * 16 + c * BLK + iota((BLK, LANES), 0), 1.0, 0.0)

    def node_terms(level, ut):
        count = ROWS >> level + 1
        listed = terms[:, sub_start(level) : sub_start(level) + count]

        def step(i, carry):
            both = lax.dot_general(listed, chosen(level, i), NT, preferred_element_type=F32)
            total = (both[:RHS] + both[RHS:]) * -weight_scale(level)
            for k in range(2):
                q = 2 * i + k
                at = q % NX * 2 + q // NX if level == 1 else q
                ut[at] = total[:, k * LANES : (k + 1) * LANES]
            return carry

        lax.fori_loop(0, (ROWS >> level) // 256, step, 0)
        own = lax.dot_general(rhs_sep[level], mark, TN, precision=lax.Precision.HIGHEST, preferred_element_type=F32)
        ut[own_chunk[level]] = ut[own_chunk[level]] + own

    mine = pl.ds(pl.multiple_of(c * LANES, LANES), LANES)
    other = pl.ds(pl.multiple_of((1 - c) * LANES, LANES), LANES)
    cols = pl.ds(pl.multiple_of(z * COLS, COLS), COLS)
    spread = pl.ds(pl.multiple_of(c * LANES + z * COLS, COLS), COLS)

    def add_own(total, own):
        def step(i, carry):
            total[i] = total[i] + own[i, mine, :]
            return carry

        lax.fori_loop(0, total.shape[0], step, 0)

    def z_stage(summed, parts):
        return [
            send(summed.at[pl.ds(pl.multiple_of(zs(d) * COLS, COLS), COLS), :], parts.at[d - 1], device(x, y, zs(d), c))
            for d in range(1, NZ)
        ]

    def z_sum(summed, parts, batch):
        arrive(batch)
        total = summed[cols, :]
        for d in range(NZ - 1):
            total = total + parts[d]
        return total

    pieces = [(2, i) for i in range(2)] + [(1, i) for i in range(4)] + [(0, i) for i in range(8)]

    def work(amount):
        for _ in range(amount):
            if pieces:
                level, i = pieces.pop()
                count = ROWS >> level + 1
                listed = slice(sub_start(level), sub_start(level) + count)
                at = slice(row_start(level) + i * 256, row_start(level) + i * 256 + 256)
                pick = chosen(level, i)
                moved_high[at, :] = jnp.dot(pick, update_high[listed, :], preferred_element_type=F32).astype(BF16)
                moved_low[at, :] = jnp.dot(pick, update_low[listed, :], preferred_element_type=F32).astype(BF16)

    coupling_terms(2)
    node_terms(2, ut2)
    c2 = send(ut2.at[:, other, :], b2c, sibling)
    coupling_terms(1)
    node_terms(1, ut1)
    c1 = send(ut1.at[:, other, :], b1c, sibling)
    c2.wait_recv()
    add_own(b2c, ut2)
    x2s = [send(b2c.at[xs(a)], b2x.at[a - 1], device(xs(a), y, z, c)) for a in range(1, NX)]
    coupling_terms(0)
    ring_step()
    c1.wait_recv()
    add_own(b1c, ut1)
    x1s = [send(b1c.at[pl.ds(xs(a) * 2, 2)], b1x.at[a - 1], device(xs(a), y, z, c)) for a in range(1, NX)]
    node_terms(0, ut0)
    c0 = send(ut0.at[:, other, :], b0c, sibling)

    arrive(x2s)
    b2s[...] = b2c[x] + b2x[0] + b2x[1] + b2x[2]
    z2s = z_stage(b2s, b2z)
    c0.wait_recv()
    add_own(b0c, ut0)
    y0s = [send(b0c.at[pl.ds(ys(b) * NX, NX)], b0y.at[b - 1], device(x, ys(b), z, c)) for b in range(1, NY)]
    ring_step()
    work(1)
    arrive(x1s)
    for i in range(2):
        b1s[i] = b1c[x * 2 + i] + b1x[0, i] + b1x[1, i] + b1x[2, i]
    y1s = send(b1s.at[1 - yy], b1y, device(x, partner, z, c))

    r2 = z_sum(b2s, b2z, z2s)
    g2[x] = r2
    a2 = [send(g2.at[x], g2.at[x], device(xs(a), y, z, c)) for a in range(1, NX)]
    work(1)
    y1s.wait_recv()
    b1t[...] = b1s[yy] + b1y[...]
    z1s = z_stage(b1t, b1z)
    work(1)
    ring_step()
    arrive(shared)

    def joined(ref):
        return jnp.concatenate([ref[i] for i in range(ref.shape[0])], axis=1)

    def spill(value, ref):
        for i in range(ref.shape[0]):
            ref[i] = value[:, i * LANES : (i + 1) * LANES]

    def columns(start, size):
        return m_ref[:, :, :, start : start + size].reshape(LANES, size)

    here1 = yy * NX + x
    here0 = y * NX + x

    def scatter_half(part, landed):
        return [
            send(part.at[(yy if b == 0 else 1 - yy) * NX + xs(a)], landed.at[k], device(xs(a), pair_y(b), z, c))
            for k, (a, b) in enumerate(half)
        ]

    def gather_half(whole):
        return [send(whole.at[here1], whole.at[here1], device(xs(a), pair_y(b), z, c)) for a, b in half]

    def scatter_plane(part, landed):
        return [
            send(part.at[ys(b) * NX + xs(a)], landed.at[k], device(xs(a), ys(b), z, c))
            for k, (a, b) in enumerate(plane)
        ]

    def gather_plane(whole):
        return [send(whole.at[here0], whole.at[here0], device(xs(a), ys(b), z, c)) for a, b in plane]

    def summed(part, here, landed, batch):
        arrive(batch)
        total = part[here]
        for k in range(landed.shape[0]):
            total = total + landed[k]
        return total

    s0_scale, s1_scale = weight_scale(0), weight_scale(1)

    arrive(a2)
    solved2 = small_dot(joined(g2), columns(G2, 512), NT)
    spill(small_dot(solved2, columns(E21, 1024), NN), p1)
    batch = scatter_half(p1, p1r)
    work(1)
    arrive(y0s)
    for i in range(NX):
        b0s[i] = b0c[y * NX + i] + b0y[0, i] + b0y[1, i] + b0y[2, i]
    x0s = [send(b0s.at[xs(a)], b0x.at[a - 1], device(xs(a), y, z, c)) for a in range(1, NX)]
    r1 = z_sum(b1t, b1z, z1s)
    g1[here1] = r1 - s1_scale * summed(p1, here1, p1r, batch)
    batch = gather_half(g1)
    up0 = small_dot(solved2, columns(E20, 2048), NN)
    work(1)
    arrive(x0s)
    b0t[...] = b0s[x] + b0x[0] + b0x[1] + b0x[2]
    z0s = z_stage(b0t, b0z)
    arrive(batch)
    solved1 = small_dot(joined(g1), columns(G1, 1024), NT)
    spill(up0 + small_dot(solved1, columns(E10, 2048), NN), p0)
    batch = scatter_plane(p0, p0r)
    work(2)
    r0 = z_sum(b0t, b0z, z0s)
    g0[here0] = r0 - s0_scale * summed(p0, here0, p0r, batch)
    batch = gather_plane(g0)
    work(2)
    arrive(batch)
    solved0 = small_dot(joined(g0), columns(G0, 2048), NT)

    def hand_out(whole, result):
        result[:, spread, :] = whole[...]
        return [send(whole, result.at[:, spread, :], device(x, y, zs(d), c)) for d in range(1, NZ)]

    spill(small_dot(solved0, columns(G0, 2048), NN), q0)
    batch = scatter_plane(q0, q0r)
    work(2)
    h0[here0] = summed(q0, here0, q0r, batch)
    batch = gather_plane(h0)
    work(2)
    arrive(batch)
    d0s = hand_out(h0, x0)
    found0 = joined(h0)
    y1 = solved1 - s0_scale * small_dot(found0, columns(E10, 2048), NT)
    spill(small_dot(y1, columns(G1, 1024), NN), q1)
    batch = scatter_half(q1, q1r)
    work(2)
    y2 = solved2 - s0_scale * small_dot(found0, columns(E20, 2048), NT)
    h1[here1] = summed(q1, here1, q1r, batch)
    batch = gather_half(h1)
    work(99)
    arrive(batch)
    d1s = hand_out(h1, x1)
    y2 = y2 - s1_scale * small_dot(joined(h1), columns(E21, 1024), NT)
    spill(small_dot(y2, columns(G2, 512), NN), q2)
    batch = [send(q2.at[xs(a)], q2r.at[a - 1], device(xs(a), y, z, c)) for a in range(1, NX)]
    h2[x] = summed(q2, x, q2r, batch)
    arrive([send(h2.at[x], h2.at[x], device(xs(a), y, z, c)) for a in range(1, NX)])
    d2s = hand_out(h2, x2)

    def swap_cores(result, batch):
        arrive(batch)
        return send(result.at[:, mine, :], result.at[:, mine, :], sibling)

    def take_in(level, result, copy):
        copy.wait_recv()

        def step(i, carry):
            at = pl.ds(pl.multiple_of(row_start(level) + i * 256, 256), 256)
            both = jnp.concatenate([result[2 * i], result[2 * i + 1]], axis=1)
            high, low = split(both)
            stacked = jnp.concatenate([high, low], axis=0)
            first = jnp.dot(stacked, moved_high[at, :], preferred_element_type=F32)
            second = jnp.dot(high, moved_low[at, :], preferred_element_type=F32)
            current[...] = current[...] - weight_scale(level) * (first[:RHS] + first[RHS:] + second)
            return carry

        lax.fori_loop(0, (ROWS >> level) // 256, step, 0)
        chunk = [here0, here1, x][level]
        out_sep[level] = lax.dot_general(
            mark, result[chunk], NT, precision=lax.Precision.HIGHEST, preferred_element_type=F32
        )

    w0 = swap_cores(x0, d0s)
    w1 = swap_cores(x1, d1s)
    take_in(0, x0, w0)
    w2 = swap_cores(x2, d2s)
    take_in(1, x1, w1)
    take_in(2, x2, w2)
    out_sub[...] = small_dot(current[...] * scale, inverse[...], NN).T
    for copy in copies:
        copy.wait_send()


N_COPIES = 3 + 3 + 3 + 3 + 7 + 1 + 3 + 7 + 3 + 7 + 7 + 7 + 15 + 15 + 15 + 15 + 7 + 7 + 7 + 7 + 3 + 3 + 7 + 3 + 8 + 8


def whole(*operands):
    def piece(*lead, rows=COLS):
        return pltpu.VMEM((*lead, rows, LANES), F32)

    scratch = [
        pltpu.VMEM((LOC, LOC), F32), pltpu.VMEM((LOC, RHS), F32), pltpu.VMEM((1792, LOC), F32),
        pltpu.VMEM((LOC, LOC), F32), pltpu.VMEM((RHS, LOC), F32), pltpu.VMEM((RHS, LOC), F32),
        pltpu.VMEM((2 * RHS, 1792), BF16), pltpu.VMEM((1792, LOC), BF16), pltpu.VMEM((1792, LOC), BF16),
        pltpu.VMEM((3584, LOC), BF16), pltpu.VMEM((3584, LOC), BF16),
        piece(16, rows=RHS), piece(8, rows=RHS), piece(4, rows=RHS),
        pltpu.VMEM((NZ, 2, BLK, WIDE), F32),
        piece(16, rows=RHS), piece(8, rows=RHS), piece(4, rows=RHS),
        piece(4, rows=LANES), piece(8, rows=LANES), piece(16, rows=LANES),
        piece(3, rows=LANES), piece(rows=LANES), piece(7),
        piece(3, 2, rows=LANES), piece(2, rows=LANES), piece(rows=LANES), piece(rows=LANES), piece(7),
        piece(3, 4, rows=LANES), piece(4, rows=LANES), piece(3, rows=LANES), piece(rows=LANES), piece(7),
        piece(4), piece(8), piece(7), piece(8), piece(16), piece(15), piece(16),
        piece(16), piece(15), piece(16), piece(8), piece(7), piece(8), piece(4), piece(3), piece(4),
        pltpu.SemaphoreType.DMA((3,)), pltpu.SemaphoreType.DMA((N_COPIES,)), pltpu.SemaphoreType.DMA((N_COPIES,)),
    ]
    vmem = pl.BlockSpec(memory_space=pltpu.VMEM)
    hbm = pl.BlockSpec(memory_space=pl.ANY)
    return pl.pallas_call(
        whole_kernel,
        out_shape=[jax.ShapeDtypeStruct((LOC, RHS), F32), jax.ShapeDtypeStruct((LEVELS, BLK, RHS), F32)],
        in_specs=[vmem] * 6 + [hbm] * 3,
        out_specs=[vmem] * 2,
        scratch_shapes=scratch,
        compiler_params=pltpu.CompilerParams(
            collective_id=0, has_side_effects=True, vmem_limit_bytes=58 * 1024 * 1024
        ),
    )(*operands)


def body(rhs_sub, rhs_sep, sub_factor, sub_diag, sep_factor, sep_diag, sub_update, update_rows, sep_update):
    result_sub, result_sep = whole(
        sub_diag, update_rows, rhs_sep, sep_factor, sep_diag, sep_update[0].T, sub_factor[0], rhs_sub[0], sub_update[0]
    )
    return result_sub[None], result_sep


def solution(mesh):
    both = ("leaf", "panel")
    in_specs = (
        P(both, None, None), P(None, both, None), P(both, None, None), P(both, None), P(both, None),
        P(None, both), P(both, None, None), P(both, None), P(both, None, None),
    )
    out_specs = (P(both, None, None), P(None, both, None))
    return jax.shard_map(body, mesh=mesh, in_specs=in_specs, out_specs=out_specs, check_vma=False)
```

time: 252 us -> 131 us (0.52); the launches traced: 247 us -> 130 us
  other arithmetic: 48.7 us -> 0 us
  matrix products: 40 us -> 0 us
  local copies, waits for them, and re-layouts: 32.1 us -> 3.21 us
  Pallas kernels: 105 us -> 126 us
  between operations: 15.3 us -> 0.64 us
  blocking collectives: 5.19 us -> 0 us
    another operation x4 -> x0, other arithmetic: 40.2 us -> none  [the longest x3 39.5 us: solve_lower(): lax.linalg.triangular_solve(matrix, right_side, left_side=True, lower=Tru...]
    dot_general x27 -> x0, matrix products: 32.9 us -> none  [the longest x12 17.4 us: exact_right_dot(): return dot(lh, right) + dot(ll, right)]
    pallas_call x1, Pallas kernels: 105 us -> 126 us  [whole(): pl.pallas_call(whole_kernel, out_shape=[jax.ShapeDtypeStruct((LOC, RHS),...]
    reshape x5 -> x0, local copies, waits for them, and re-layouts: 8.26 us -> none  [the longest x1 3.34 us: reorder_columns(): return jnp.swapaxes(value, 2, 3).reshape(lead, width)]
    another operation x13 -> x0, local copies, waits for them, and re-layouts: 7.83 us -> none
    another operation x14 -> x0, matrix products: 7.08 us -> none  [solve_lower(): lax.linalg.triangular_solve(matrix, right_side, left_side=True, lower=Tru...]
    transpose x4 -> x0, local copies, waits for them, and re-layouts: 7.01 us -> none  [the longest x3 5.4 us: body(): whole = found[level].swapaxes(0, 1).reshape(RHS, node_rows)]
    all_gather x1 -> x0, blocking collectives: 5.19 us -> none  [body(): lax.all_gather(matrix, 'panel', axis=0, tiled=True, axis_index_groups=pairs)]
  transfers between devices with their start and end apart: 1 -> 0, of which waited for: 0 -> 0; matrix products, arithmetic and copies ran while one was open for 29% -> 0% of each run, Pallas kernels for 0% -> 0%
where the time goes in v2:
time: 131 us; the launch traced here: 130 us
  Pallas kernels  126 us (96%)
  local copies, waits for them, and re-layouts  3.21 us (2%)
    pallas_call x1, Pallas kernels, whole(): pl.pallas_call(whole_kernel, out_shape=[jax.ShapeDtypeStruct((LOC, RHS),...  126 us
    unnamed x2, local copies, waits for them, and re-layouts  3.21 us

profile of v2, /device:TPU:1, one launch (start us, length us, event | category | flops | bytes accessed | tf_op | source)
XLA Modules:
  0.0 130.3 jit_solution(4754943541500713064)
XLA Ops:
  0.6 126.5 %shard_map.104 = (f32[512,256]{1,0:T(8,128)}, f32[3,8,256]{2,1,0:T(8,128)}) custom-call(f32[1,512]{1,0:T(1,128)} %diag.1, s32[1,1792]{1,0:T(1,128)} %rows.1, f32[3,8,256]{2,1,0:T(8,128)} %rhs_sep.1, f32[8,3584]{1,0:T(8,128)} %sep_factor.1, f32[3,8]{1,0:T(4,128)} %sep_diag.1, f32[8,5120]{1,0:T(8,128)} %bitcast.11, f32[512,512]{1,0:T(8,128)} %bitcast.8, ...), custom_call_target="tpu_custom_call" | custom-call | tf_op jit(solution)/shard_map/pallas_call | solution.py:522
  127.1 1.9 %copy.13 = f32[1,512,256]{2,1,0:T(8,128)} copy(f32[1,512,256]{2,1,0:T(8,128)} %bitcast.9) | data formatting | bytes 1048576
  129.0 1.3 %copy.14 = f32[3,8,256]{2,1,0:T(8,128)} copy(f32[3,8,256]{2,1,0:T(8,128)} %get-tuple-element.9) | data formatting | bytes 49152

commit v3 on v2

--- a/solution.py
+++ b/solution.py
@@ -47,6 +47,20 @@
 
 def device(x, y, z, c):
     return (y * NZ + z, x * 2 + c)
+
+
+def hops(step, size):
+    return min(step, size - step)
+
+
+X_PEERS = (2, 1, 3)
+Y_PEERS = (2, 1, 3)
+Z_PEERS = (4, 3, 5, 2, 6, 1, 7)
+PLANE = sorted(
+    [(a, b) for a in range(NX) for b in range(NY)][1:], key=lambda ab: -hops(ab[0], NX) - hops(ab[1], NY)
+)
+HALF = sorted([(a, b) for a in range(NX) for b in range(2)][1:], key=lambda ab: -hops(ab[0], NX) - ab[1])
+ROUNDS = ((0, 1536), (1536, 4608), (4608, 8704))
 
 
 def split3(value):
@@ -142,7 +156,7 @@
     out_sub, out_sep,
     factor, rhs, update, inverse, solved_t, current, terms, update_high, update_low, moved_high, moved_low,
     ut0, ut1, ut2, m_ref, x0, x1, x2,
-    b2c, b1c, b0c, b2x, b2s, b2z, b1x, b1s, b1y, b1t, b1z, b0y, b0s, b0x, b0t, b0z,
+    b2c, b1c, b0c, b2x, b2s, b2z, b1x, b1s, b1y, b1t, b1z, b0y, b0x, b0p, b0q, b0u, b0v, b0t, b0z,
     g2, p1, p1r, g1, p0, p0r, g0, q0, q0r, h0, q1, q1r, h1, q2, q2r, h2,
     lsem, ssem, rsem,
 ):
@@ -151,9 +165,6 @@
     partner = y + 1 - 2 * (y % 2)
     yy = y % 2
     sibling = device(x, y, z, 1 - c)
-    plane = [(a, b) for a in range(NX) for b in range(NY)][1:]
-    half = [(a, b) for a in range(NX) for b in range(2)][1:]
-
     loads = [
         pltpu.make_async_copy(src, dst, lsem.at[i])
         for i, (src, dst) in enumerate(((factor_hbm, factor), (rhs_hbm, rhs), (update_hbm, update)))
@@ -174,7 +185,7 @@
         return partner if b else y
 
     barrier = pltpu.get_barrier_semaphore()
-    greeted = [device(xs(a), ys(b), z, c) for a, b in plane]
+    greeted = [device(xs(a), ys(b), z, c) for a, b in PLANE]
     greeted += [device(x, y, zs(d), c) for d in range(1, NZ)] + [sibling]
     for peer in greeted:
         pl.semaphore_signal(barrier, inc=1, device_id=peer, device_id_type=MESH)
@@ -200,30 +211,33 @@
         m_ref[z, c, :, i * 512 : (i + 1) * 512] = own_rows[i * BLK : (i + 1) * BLK]
     pl.semaphore_wait(barrier, len(greeted))
 
-    def pass_on(block, columns, peer):
-        ref = m_ref.at[block, c, :, columns]
+    right, left = device(x, y, zs(1), c), device(x, y, zs(NZ - 1), c)
+
+    def pass_on(block, start, size, peer):
+        ref = m_ref.at[block, c, :, pl.ds(start, size)]
         return send(ref, ref, peer)
 
-    everything, front, back = pl.ds(0, WIDE), pl.ds(0, WIDE // 2), pl.ds(WIDE // 2, WIDE // 2)
-    right, left = device(x, y, zs(1), c), device(x, y, zs(NZ - 1), c)
-    ring = [[pass_on(z, everything, right), pass_on(z, everything, left)]]
-    shared = [pass_on(z, everything, sibling)]
-
-    def ring_step():
-        step = len(ring)
-        arrive(ring[-1])
+    ring, steps, shared = [], [1] * len(ROUNDS), [None] * len(ROUNDS)
+    for start, stop in ROUNDS:
+        ring.append([pass_on(z, start, stop - start, right), pass_on(z, start, stop - start, left)])
+
+    def advance(turn):
+        step = steps[turn]
+        steps[turn] = step + 1
+        start, stop = ROUNDS[turn]
+        size = stop - start
         from_left, from_right = zs(NZ - step), zs(step)
+        arrive(ring[turn])
         if step < 3:
-            ring.append([pass_on(from_left, everything, right), pass_on(from_right, everything, left)])
+            ring[turn] = [pass_on(from_left, start, size, right), pass_on(from_right, start, size, left)]
         elif step == 3:
-            ring.append([pass_on(from_left, front, right), pass_on(from_right, back, left)])
+            ring[turn] = [
+                pass_on(from_left, start, size // 2, right),
+                pass_on(from_right, start + size // 2, size // 2, left),
+            ]
         else:
-            ring.append([])
-        if step < 4:
-            shared.append(pass_on(from_left, everything, sibling))
-            shared.append(pass_on(from_right, everything, sibling))
-        else:
-            shared.append(pass_on(from_left, everything, sibling))
+            ref = m_ref.at[:, c, :, pl.ds(start, size)]
+            shared[turn] = [send(ref, ref, sibling)]
 
     scale = 1.0 / diag[...]
     loads[0].wait()
@@ -232,7 +246,7 @@
     right_t = rhs[...].T
     solved_t[...] = small_dot(right_t, inverse[...], NT) * scale
     current[...] = solved_t[...]
-    ring_step()
+    advance(0)
     loads[2].wait()
     solved_high, solved_low = split(solved_t[...])
     solved_both = jnp.concatenate([solved_high, solved_low], axis=0)
@@ -262,10 +276,9 @@
         ids = iota((256, count), 0) + i * 256
         return jnp.where(ids == places[level], 1.0, 0.0).astype(BF16)
 
-    own_chunk = [y * NX + x, x * 2 + yy, x]
     mark = jnp.where(iota((BLK, LANES), 1) == z * 16 + c * BLK + iota((BLK, LANES), 0), 1.0, 0.0)
 
-    def node_terms(level, ut):
+    def node_terms(level, ut, first, last):
         count = ROWS >> level + 1
         listed = terms[:, sub_start(level) : sub_start(level) + count]
 
@@ -273,14 +286,21 @@
             both = lax.dot_general(listed, chosen(level, i), NT, preferred_element_type=F32)
             total = (both[:RHS] + both[RHS:]) * -weight_scale(level)
             for k in range(2):
-                q = 2 * i + k
-                at = q % NX * 2 + q // NX if level == 1 else q
-                ut[at] = total[:, k * LANES : (k + 1) * LANES]
+                part = total[:, k * LANES : (k + 1) * LANES]
+                if level == 0:
+                    ut[i // 2, i % 2 * 2 + k] = part
+                elif level == 1:
+                    ut[(i % 2 * 2 + k) * 2 + i // 2] = part
+                else:
+                    ut[2 * i + k] = part
             return carry
 
-        lax.fori_loop(0, (ROWS >> level) // 256, step, 0)
-        own = lax.dot_general(rhs_sep[level], mark, TN, precision=lax.Precision.HIGHEST, preferred_element_type=F32)
-        ut[own_chunk[level]] = ut[own_chunk[level]] + own
+        lax.fori_loop(first, last, step, 0)
+
+    def own_term(level):
+        return lax.dot_general(
+            rhs_sep[level], mark, TN, precision=lax.Precision.HIGHEST, preferred_element_type=F32
+        )
 
     mine = pl.ds(pl.multiple_of(c * LANES, LANES), LANES)
     other = pl.ds(pl.multiple_of((1 - c) * LANES, LANES), LANES)
@@ -297,7 +317,7 @@
     def z_stage(summed, parts):
         return [
             send(summed.at[pl.ds(pl.multiple_of(zs(d) * COLS, COLS), COLS), :], parts.at[d - 1], device(x, y, zs(d), c))
-            for d in range(1, NZ)
+            for d in Z_PEERS
         ]
 
     def z_sum(summed, parts, batch):
@@ -320,46 +340,76 @@
                 moved_high[at, :] = jnp.dot(pick, update_high[listed, :], preferred_element_type=F32).astype(BF16)
                 moved_low[at, :] = jnp.dot(pick, update_low[listed, :], preferred_element_type=F32).astype(BF16)
 
+    def x_send(piece, landed):
+        return [send(piece(xs(a)), landed.at[a - 1], device(xs(a), y, z, c)) for a in X_PEERS]
+
+    def y_send(piece, landed):
+        return [send(piece(ys(b)), landed.at[b - 1], device(x, ys(b), z, c)) for b in Y_PEERS]
+
     coupling_terms(2)
-    node_terms(2, ut2)
+    node_terms(2, ut2, 0, 2)
+    ut2[x] = ut2[x] + own_term(2)
     c2 = send(ut2.at[:, other, :], b2c, sibling)
+    advance(1)
     coupling_terms(1)
-    node_terms(1, ut1)
+    node_terms(1, ut1, 0, 4)
+    ut1[x * 2 + yy] = ut1[x * 2 + yy] + own_term(1)
     c1 = send(ut1.at[:, other, :], b1c, sibling)
-    c2.wait_recv()
+    arrive([c2])
     add_own(b2c, ut2)
-    x2s = [send(b2c.at[xs(a)], b2x.at[a - 1], device(xs(a), y, z, c)) for a in range(1, NX)]
+    x2s = x_send(lambda to: b2c.at[to], b2x)
+    advance(0)
     coupling_terms(0)
-    ring_step()
-    c1.wait_recv()
+    advance(2)
+    arrive([c1])
     add_own(b1c, ut1)
-    x1s = [send(b1c.at[pl.ds(xs(a) * 2, 2)], b1x.at[a - 1], device(xs(a), y, z, c)) for a in range(1, NX)]
-    node_terms(0, ut0)
-    c0 = send(ut0.at[:, other, :], b0c, sibling)
-
+    x1s = x_send(lambda to: b1c.at[pl.ds(to * 2, 2)], b1x)
+    node_terms(0, ut0, 0, 2)
+    advance(1)
+    node_terms(0, ut0, 2, 4)
+    lower = jnp.where(y < 2, 1.0, 0.0)
+    own0 = own_term(0)
+    ut0[y % 2, x] = ut0[y % 2, x] + own0 * lower
+    c0a = send(ut0.at[0:2, :, other, :], b0c.at[0:2], sibling)
+    advance(0)
     arrive(x2s)
     b2s[...] = b2c[x] + b2x[0] + b2x[1] + b2x[2]
     z2s = z_stage(b2s, b2z)
-    c0.wait_recv()
-    add_own(b0c, ut0)
-    y0s = [send(b0c.at[pl.ds(ys(b) * NX, NX)], b0y.at[b - 1], device(x, ys(b), z, c)) for b in range(1, NY)]
-    ring_step()
-    work(1)
+    node_terms(0, ut0, 4, 6)
+    advance(2)
+    node_terms(0, ut0, 6, 8)
+    ut0[2 + y % 2, x] = ut0[2 + y % 2, x] + own0 * (1.0 - lower)
+    c0b = send(ut0.at[2:4, :, other, :], b0c.at[2:4], sibling)
+    advance(1)
+
+    def add_rows(first):
+        def step(i, carry):
+            for k in range(NX):
+                b0c[first + i, k] = b0c[first + i, k] + ut0[first + i, k, mine, :]
+            return carry
+
+        lax.fori_loop(0, 2, step, 0)
+
+    arrive([c0a])
+    add_rows(0)
+    arrive([c0b])
+    add_rows(2)
+    mid = LANES // 2
+    y0s = y_send(lambda to: b0c.at[to, :, 0:mid, :], b0y)
+    x0s = x_send(lambda to: b0c.at[:, to, mid:LANES, :], b0x)
+    advance(0)
+    r2 = z_sum(b2s, b2z, z2s)
+    g2[x] = r2
+    a2 = [send(g2.at[x], g2.at[x], device(xs(a), y, z, c)) for a in X_PEERS]
+    advance(2)
     arrive(x1s)
     for i in range(2):
         b1s[i] = b1c[x * 2 + i] + b1x[0, i] + b1x[1, i] + b1x[2, i]
     y1s = send(b1s.at[1 - yy], b1y, device(x, partner, z, c))
-
-    r2 = z_sum(b2s, b2z, z2s)
-    g2[x] = r2
-    a2 = [send(g2.at[x], g2.at[x], device(xs(a), y, z, c)) for a in range(1, NX)]
     work(1)
-    y1s.wait_recv()
+    arrive([y1s])
     b1t[...] = b1s[yy] + b1y[...]
     z1s = z_stage(b1t, b1z)
-    work(1)
-    ring_step()
-    arrive(shared)
 
     def joined(ref):
         return jnp.concatenate([ref[i] for i in range(ref.shape[0])], axis=1)
@@ -377,20 +427,20 @@
     def scatter_half(part, landed):
         return [
             send(part.at[(yy if b == 0 else 1 - yy) * NX + xs(a)], landed.at[k], device(xs(a), pair_y(b), z, c))
-            for k, (a, b) in enumerate(half)
+            for k, (a, b) in enumerate(HALF)
         ]
 
     def gather_half(whole):
-        return [send(whole.at[here1], whole.at[here1], device(xs(a), pair_y(b), z, c)) for a, b in half]
+        return [send(whole.at[here1], whole.at[here1], device(xs(a), pair_y(b), z, c)) for a, b in HALF]
 
     def scatter_plane(part, landed):
         return [
             send(part.at[ys(b) * NX + xs(a)], landed.at[k], device(xs(a), ys(b), z, c))
-            for k, (a, b) in enumerate(plane)
+            for k, (a, b) in enumerate(PLANE)
         ]
 
     def gather_plane(whole):
-        return [send(whole.at[here0], whole.at[here0], device(xs(a), ys(b), z, c)) for a, b in plane]
+        return [send(whole.at[here0], whole.at[here0], device(xs(a), ys(b), z, c)) for a, b in PLANE]
 
     def summed(part, here, landed, batch):
         arrive(batch)
@@ -401,71 +451,100 @@
 
     s0_scale, s1_scale = weight_scale(0), weight_scale(1)
 
+    arrive(shared[0])
     arrive(a2)
     solved2 = small_dot(joined(g2), columns(G2, 512), NT)
     spill(small_dot(solved2, columns(E21, 1024), NN), p1)
-    batch = scatter_half(p1, p1r)
+    p1s = scatter_half(p1, p1r)
+    advance(1)
     work(1)
     arrive(y0s)
     for i in range(NX):
-        b0s[i] = b0c[y * NX + i] + b0y[0, i] + b0y[1, i] + b0y[2, i]
-    x0s = [send(b0s.at[xs(a)], b0x.at[a - 1], device(xs(a), y, z, c)) for a in range(1, NX)]
+        b0p[i] = b0c[y, i, 0:mid, :] + b0y[0, i] + b0y[1, i] + b0y[2, i]
+    x0t = x_send(lambda to: b0p.at[to], b0u)
+    arrive(x0s)
+    for i in range(NY):
+        b0q[i] = b0c[i, x, mid:LANES, :] + b0x[0, i] + b0x[1, i] + b0x[2, i]
+    y0t = y_send(lambda to: b0q.at[to], b0v)
     r1 = z_sum(b1t, b1z, z1s)
-    g1[here1] = r1 - s1_scale * summed(p1, here1, p1r, batch)
-    batch = gather_half(g1)
+    g1[here1] = r1 - s1_scale * summed(p1, here1, p1r, p1s)
+    a1 = gather_half(g1)
+    arrive(shared[1])
     up0 = small_dot(solved2, columns(E20, 2048), NN)
-    work(1)
-    arrive(x0s)
-    b0t[...] = b0s[x] + b0x[0] + b0x[1] + b0x[2]
+    advance(2)
+    arrive(x0t)
+    b0t[0:mid, :] = b0p[x] + b0u[0] + b0u[1] + b0u[2]
+    arrive(y0t)
+    b0t[mid:LANES, :] = b0q[y] + b0v[0] + b0v[1] + b0v[2]
     z0s = z_stage(b0t, b0z)
-    arrive(batch)
+    arrive(a1)
     solved1 = small_dot(joined(g1), columns(G1, 1024), NT)
+    arrive(shared[2])
     spill(up0 + small_dot(solved1, columns(E10, 2048), NN), p0)
-    batch = scatter_plane(p0, p0r)
+    p0s = scatter_plane(p0, p0r)
     work(2)
     r0 = z_sum(b0t, b0z, z0s)
-    g0[here0] = r0 - s0_scale * summed(p0, here0, p0r, batch)
-    batch = gather_plane(g0)
+    g0[here0] = r0 - s0_scale * summed(p0, here0, p0r, p0s)
+    a0 = gather_plane(g0)
     work(2)
-    arrive(batch)
+    arrive(a0)
     solved0 = small_dot(joined(g0), columns(G0, 2048), NT)
 
-    def hand_out(whole, result):
-        result[:, spread, :] = whole[...]
-        return [send(whole, result.at[:, spread, :], device(x, y, zs(d), c)) for d in range(1, NZ)]
+    def block_of(d):
+        return pl.ds(pl.multiple_of(c * LANES + zs(d) * COLS, COLS), COLS)
+
+    def along_z(chunk, at, result):
+        result[at, spread, :] = chunk[at]
+        return [send(chunk.at[at], result.at[at, spread, :], device(x, y, zs(d), c)) for d in Z_PEERS]
 
     spill(small_dot(solved0, columns(G0, 2048), NN), q0)
-    batch = scatter_plane(q0, q0r)
+    q0s = scatter_plane(q0, q0r)
     work(2)
-    h0[here0] = summed(q0, here0, q0r, batch)
-    batch = gather_plane(h0)
+    h0[here0] = summed(q0, here0, q0r, q0s)
+    a0 = gather_plane(h0)
     work(2)
-    arrive(batch)
-    d0s = hand_out(h0, x0)
+    arrive(a0)
+    x0[:, spread, :] = h0[...]
+    far0, near0 = [
+        [send(h0, x0.at[:, spread, :], device(x, y, zs(d), c)) for d in ds] for ds in ((2, 6), (1, 7))
+    ]
     found0 = joined(h0)
     y1 = solved1 - s0_scale * small_dot(found0, columns(E10, 2048), NT)
     spill(small_dot(y1, columns(G1, 1024), NN), q1)
-    batch = scatter_half(q1, q1r)
+    q1s = scatter_half(q1, q1r)
+    y2 = solved2 - s0_scale * small_dot(found0, columns(E20, 2048), NT)
+    work(1)
+    h1[here1] = summed(q1, here1, q1r, q1s)
+    a1 = gather_half(h1)
+    z1h = along_z(h1, here1, x1)
     work(2)
-    y2 = solved2 - s0_scale * small_dot(found0, columns(E20, 2048), NT)
-    h1[here1] = summed(q1, here1, q1r, batch)
-    batch = gather_half(h1)
-    work(99)
-    arrive(batch)
-    d1s = hand_out(h1, x1)
+    arrive(a1)
     y2 = y2 - s1_scale * small_dot(joined(h1), columns(E21, 1024), NT)
     spill(small_dot(y2, columns(G2, 512), NN), q2)
-    batch = [send(q2.at[xs(a)], q2r.at[a - 1], device(xs(a), y, z, c)) for a in range(1, NX)]
-    h2[x] = summed(q2, x, q2r, batch)
-    arrive([send(h2.at[x], h2.at[x], device(xs(a), y, z, c)) for a in range(1, NX)])
-    d2s = hand_out(h2, x2)
+    q2s = x_send(lambda to: q2.at[to], q2r)
+    arrive(far0)
+    low, high = block_of(6), block_of(2)
+    far0 = [
+        send(x0.at[:, low, :], x0.at[:, low, :], device(x, y, zs(1), c)),
+        send(x0.at[:, high, :], x0.at[:, high, :], device(x, y, zs(7), c)),
+        send(x0.at[0:8, low, :], x0.at[0:8, low, :], device(x, y, zs(2), c)),
+        send(x0.at[8:16, high, :], x0.at[8:16, high, :], device(x, y, zs(6), c)),
+    ]
+    h2[x] = summed(q2, x, q2r, q2s)
+    z2h = along_z(h2, x, x2)
+    arrive(z1h)
+    w1 = [send(x1.at[here1, mine, :], x1.at[here1, mine, :], device(xs(a), pair_y(b), z, c)) for a, b in HALF]
+    work(99)
+    arrive(near0)
+    arrive(z2h)
+    w2 = [send(x2.at[x, mine, :], x2.at[x, mine, :], device(xs(a), y, z, c)) for a in X_PEERS]
 
     def swap_cores(result, batch):
         arrive(batch)
         return send(result.at[:, mine, :], result.at[:, mine, :], sibling)
 
     def take_in(level, result, copy):
-        copy.wait_recv()
+        arrive([copy])
 
         def step(i, carry):
             at = pl.ds(pl.multiple_of(row_start(level) + i * 256, 256), 256)
@@ -483,10 +562,10 @@
             mark, result[chunk], NT, precision=lax.Precision.HIGHEST, preferred_element_type=F32
         )
 
-    w0 = swap_cores(x0, d0s)
-    w1 = swap_cores(x1, d1s)
+    w0 = swap_cores(x0, far0)
     take_in(0, x0, w0)
-    w2 = swap_cores(x2, d2s)
+    w1 = swap_cores(x1, w1)
+    w2 = swap_cores(x2, w2)
     take_in(1, x1, w1)
     take_in(2, x2, w2)
     out_sub[...] = small_dot(current[...] * scale, inverse[...], NN).T
@@ -494,7 +573,7 @@
         copy.wait_send()
 
 
-N_COPIES = 3 + 3 + 3 + 3 + 7 + 1 + 3 + 7 + 3 + 7 + 7 + 7 + 15 + 15 + 15 + 15 + 7 + 7 + 7 + 7 + 3 + 3 + 7 + 3 + 8 + 8
+N_COPIES = 256
 
 
 def whole(*operands):
@@ -506,13 +585,14 @@
         pltpu.VMEM((LOC, LOC), F32), pltpu.VMEM((RHS, LOC), F32), pltpu.VMEM((RHS, LOC), F32),
         pltpu.VMEM((2 * RHS, 1792), BF16), pltpu.VMEM((1792, LOC), BF16), pltpu.VMEM((1792, LOC), BF16),
         pltpu.VMEM((3584, LOC), BF16), pltpu.VMEM((3584, LOC), BF16),
-        piece(16, rows=RHS), piece(8, rows=RHS), piece(4, rows=RHS),
+        piece(4, 4, rows=RHS), piece(8, rows=RHS), piece(4, rows=RHS),
         pltpu.VMEM((NZ, 2, BLK, WIDE), F32),
         piece(16, rows=RHS), piece(8, rows=RHS), piece(4, rows=RHS),
-        piece(4, rows=LANES), piece(8, rows=LANES), piece(16, rows=LANES),
+        piece(4, rows=LANES), piece(8, rows=LANES), piece(4, 4, rows=LANES),
         piece(3, rows=LANES), piece(rows=LANES), piece(7),
         piece(3, 2, rows=LANES), piece(2, rows=LANES), piece(rows=LANES), piece(rows=LANES), piece(7),
-        piece(3, 4, rows=LANES), piece(4, rows=LANES), piece(3, rows=LANES), piece(rows=LANES), piece(7),
+        piece(3, 4, rows=64), piece(3, 4, rows=64), piece(4, rows=64), piece(4, rows=64),
+        piece(3, rows=64), piece(3, rows=64), piece(rows=LANES), piece(7),
         piece(4), piece(8), piece(7), piece(8), piece(16), piece(15), piece(16),
         piece(16), piece(15), piece(16), piece(8), piece(7), piece(8), piece(4), piece(3), piece(4),
         pltpu.SemaphoreType.DMA((3,)), pltpu.SemaphoreType.DMA((N_COPIES,)), pltpu.SemaphoreType.DMA((N_COPIES,)),

time: 131 us -> 109 us (0.83)
  Pallas kernels: 126 us -> 104 us
    pallas_call x1, Pallas kernels: 126 us -> 104 us  [whole(): pl.pallas_call(whole_kernel, out_shape=[jax.ShapeDtypeStruct((LOC, RHS),...]
where the time goes in v3:
time: 109 us; the launch traced here: 108 us
  Pallas kernels  104 us (95%)
  local copies, waits for them, and re-layouts  3.21 us (3%)
    pallas_call x1, Pallas kernels, whole(): pl.pallas_call(whole_kernel, out_shape=[jax.ShapeDtypeStruct((LOC, RHS),...  104 us
    unnamed x2, local copies, waits for them, and re-layouts  3.21 us

profile of v3, /device:TPU:1, one launch (start us, length us, event | category | flops | bytes accessed | tf_op | source)
XLA Modules:
  0.0 107.9 jit_solution(5298680286933277629)
XLA Ops:
  0.6 104.1 %shard_map.104 = (f32[512,256]{1,0:T(8,128)}, f32[3,8,256]{2,1,0:T(8,128)}) custom-call(f32[1,512]{1,0:T(1,128)} %diag.1, s32[1,1792]{1,0:T(1,128)} %rows.1, f32[3,8,256]{2,1,0:T(8,128)} %rhs_sep.1, f32[8,3584]{1,0:T(8,128)} %sep_factor.1, f32[3,8]{1,0:T(4,128)} %sep_diag.1, f32[8,5120]{1,0:T(8,128)} %bitcast.11, f32[512,512]{1,0:T(8,128)} %bitcast.8, ...), custom_call_target="tpu_custom_call" | custom-call | tf_op jit(solution)/shard_map/pallas_call | solution.py:602
  104.7 1.9 %copy.13 = f32[1,512,256]{2,1,0:T(8,128)} copy(f32[1,512,256]{2,1,0:T(8,128)} %bitcast.9) | data formatting | bytes 1048576
  106.6 1.3 %copy.14 = f32[3,8,256]{2,1,0:T(8,128)} copy(f32[3,8,256]{2,1,0:T(8,128)} %get-tuple-element.9) | data formatting | bytes 49152

commit v4 on v3

--- a/solution.py
+++ b/solution.py
@@ -209,6 +209,15 @@
     own_rows = separator_rows(sep_factor, sep_diag, turned, position)
     for i in range(WIDE // 512):
         m_ref[z, c, :, i * 512 : (i + 1) * 512] = own_rows[i * BLK : (i + 1) * BLK]
+
+    scale = 1.0 / diag[...]
+    loads[0].wait()
+    invert(factor, scale, inverse)
+    loads[1].wait()
+    right_t = rhs[...].T
+    solved_t[...] = small_dot(right_t, inverse[...], NT) * scale
+    current[...] = solved_t[...]
+
     pl.semaphore_wait(barrier, len(greeted))
 
     right, left = device(x, y, zs(1), c), device(x, y, zs(NZ - 1), c)
@@ -239,14 +248,6 @@
             ref = m_ref.at[:, c, :, pl.ds(start, size)]
             shared[turn] = [send(ref, ref, sibling)]
 
-    scale = 1.0 / diag[...]
-    loads[0].wait()
-    invert(factor, scale, inverse)
-    loads[1].wait()
-    right_t = rhs[...].T
-    solved_t[...] = small_dot(right_t, inverse[...], NT) * scale
-    current[...] = solved_t[...]
-    advance(0)
     loads[2].wait()
     solved_high, solved_low = split(solved_t[...])
     solved_both = jnp.concatenate([solved_high, solved_low], axis=0)
@@ -350,7 +351,6 @@
     node_terms(2, ut2, 0, 2)
     ut2[x] = ut2[x] + own_term(2)
     c2 = send(ut2.at[:, other, :], b2c, sibling)
-    advance(1)
     coupling_terms(1)
     node_terms(1, ut1, 0, 4)
     ut1[x * 2 + yy] = ut1[x * 2 + yy] + own_term(1)
@@ -360,12 +360,12 @@
     x2s = x_send(lambda to: b2c.at[to], b2x)
     advance(0)
     coupling_terms(0)
-    advance(2)
+    advance(1)
     arrive([c1])
     add_own(b1c, ut1)
     x1s = x_send(lambda to: b1c.at[pl.ds(to * 2, 2)], b1x)
     node_terms(0, ut0, 0, 2)
-    advance(1)
+    advance(2)
     node_terms(0, ut0, 2, 4)
     lower = jnp.where(y < 2, 1.0, 0.0)
     own0 = own_term(0)
@@ -376,11 +376,10 @@
     b2s[...] = b2c[x] + b2x[0] + b2x[1] + b2x[2]
     z2s = z_stage(b2s, b2z)
     node_terms(0, ut0, 4, 6)
-    advance(2)
+    advance(1)
     node_terms(0, ut0, 6, 8)
     ut0[2 + y % 2, x] = ut0[2 + y % 2, x] + own0 * (1.0 - lower)
     c0b = send(ut0.at[2:4, :, other, :], b0c.at[2:4], sibling)
-    advance(1)
 
     def add_rows(first):
         def step(i, carry):
@@ -397,11 +396,12 @@
     mid = LANES // 2
     y0s = y_send(lambda to: b0c.at[to, :, 0:mid, :], b0y)
     x0s = x_send(lambda to: b0c.at[:, to, mid:LANES, :], b0x)
+    advance(2)
     advance(0)
     r2 = z_sum(b2s, b2z, z2s)
     g2[x] = r2
     a2 = [send(g2.at[x], g2.at[x], device(xs(a), y, z, c)) for a in X_PEERS]
-    advance(2)
+    advance(1)
     arrive(x1s)
     for i in range(2):
         b1s[i] = b1c[x * 2 + i] + b1x[0, i] + b1x[1, i] + b1x[2, i]
@@ -410,6 +410,7 @@
     arrive([y1s])
     b1t[...] = b1s[yy] + b1y[...]
     z1s = z_stage(b1t, b1z)
+    advance(0)
 
     def joined(ref):
         return jnp.concatenate([ref[i] for i in range(ref.shape[0])], axis=1)
@@ -451,8 +452,9 @@
 
     s0_scale, s1_scale = weight_scale(0), weight_scale(1)
 
+    arrive(a2)
+    advance(2)
     arrive(shared[0])
-    arrive(a2)
     solved2 = small_dot(joined(g2), columns(G2, 512), NT)
     spill(small_dot(solved2, columns(E21, 1024), NN), p1)
     p1s = scatter_half(p1, p1r)

time: 109 us -> 106 us (0.972)
  Pallas kernels: 104 us -> 101 us
    pallas_call x1, Pallas kernels: 104 us -> 101 us  [whole(): pl.pallas_call(whole_kernel, out_shape=[jax.ShapeDtypeStruct((LOC, RHS),...]
where the time goes in v4:
time: 106 us; the launch traced here: 105 us
  Pallas kernels  101 us (95%)
  local copies, waits for them, and re-layouts  3.21 us (3%)
    pallas_call x1, Pallas kernels, whole(): pl.pallas_call(whole_kernel, out_shape=[jax.ShapeDtypeStruct((LOC, RHS),...  101 us
    unnamed x2, local copies, waits for them, and re-layouts  3.21 us

profile of v4, /device:TPU:1, one launch (start us, length us, event | category | flops | bytes accessed | tf_op | source)
XLA Modules:
  0.0 104.6 jit_solution(10113896274942067496)
XLA Ops:
  0.6 100.8 %shard_map.104 = (f32[512,256]{1,0:T(8,128)}, f32[3,8,256]{2,1,0:T(8,128)}) custom-call(f32[1,512]{1,0:T(1,128)} %diag.1, s32[1,1792]{1,0:T(1,128)} %rows.1, f32[3,8,256]{2,1,0:T(8,128)} %rhs_sep.1, f32[8,3584]{1,0:T(8,128)} %sep_factor.1, f32[3,8]{1,0:T(4,128)} %sep_diag.1, f32[8,5120]{1,0:T(8,128)} %bitcast.11, f32[512,512]{1,0:T(8,128)} %bitcast.8, ...), custom_call_target="tpu_custom_call" | custom-call | tf_op jit(solution)/shard_map/pallas_call | solution.py:604
  101.4 1.9 %copy.13 = f32[1,512,256]{2,1,0:T(8,128)} copy(f32[1,512,256]{2,1,0:T(8,128)} %bitcast.9) | data formatting | bytes 1048576
  103.3 1.3 %copy.14 = f32[3,8,256]{2,1,0:T(8,128)} copy(f32[3,8,256]{2,1,0:T(8,128)} %get-tuple-element.9) | data formatting | bytes 49152

commit v5 on v4

--- a/solution.py
+++ b/solution.py
@@ -156,7 +156,7 @@
     out_sub, out_sep,
     factor, rhs, update, inverse, solved_t, current, terms, update_high, update_low, moved_high, moved_low,
     ut0, ut1, ut2, m_ref, x0, x1, x2,
-    b2c, b1c, b0c, b2x, b2s, b2z, b1x, b1s, b1y, b1t, b1z, b0y, b0x, b0p, b0q, b0u, b0v, b0t, b0z,
+    b2c, b1c, b0c, b2x, b2s, b2z, b1x, b1y, b1p, b1q, b1u, b1v, b1t, b1z, b0y, b0x, b0p, b0q, b0u, b0v, b0t, b0z,
     g2, p1, p1r, g1, p0, p0r, g0, q0, q0r, h0, q1, q1r, h1, q2, q2r, h2,
     lsem, ssem, rsem,
 ):
@@ -291,7 +291,7 @@
                 if level == 0:
                     ut[i // 2, i % 2 * 2 + k] = part
                 elif level == 1:
-                    ut[(i % 2 * 2 + k) * 2 + i // 2] = part
+                    ut[i % 2 * 2 + k, i // 2] = part
                 else:
                     ut[2 * i + k] = part
             return carry
@@ -352,34 +352,42 @@
     ut2[x] = ut2[x] + own_term(2)
     c2 = send(ut2.at[:, other, :], b2c, sibling)
     coupling_terms(1)
-    node_terms(1, ut1, 0, 4)
-    ut1[x * 2 + yy] = ut1[x * 2 + yy] + own_term(1)
-    c1 = send(ut1.at[:, other, :], b1c, sibling)
     arrive([c2])
     add_own(b2c, ut2)
     x2s = x_send(lambda to: b2c.at[to], b2x)
+    node_terms(1, ut1, 0, 4)
+    ut1[x, yy] = ut1[x, yy] + own_term(1)
+    c1 = send(ut1.at[:, :, other, :], b1c, sibling)
     advance(0)
     coupling_terms(0)
+    mid = LANES // 2
+    arrive([c1])
+
+    def add_pair(i, carry):
+        for k in range(2):
+            b1c[i, k] = b1c[i, k] + ut1[i, k, mine, :]
+        return carry
+
+    lax.fori_loop(0, NX, add_pair, 0)
+    x1s = x_send(lambda to: b1c.at[to, :, 0:mid, :], b1x)
+    y1s = send(b1c.at[:, 1 - yy, mid:LANES, :], b1y, device(x, partner, z, c))
     advance(1)
-    arrive([c1])
-    add_own(b1c, ut1)
-    x1s = x_send(lambda to: b1c.at[pl.ds(to * 2, 2)], b1x)
     node_terms(0, ut0, 0, 2)
-    advance(2)
     node_terms(0, ut0, 2, 4)
     lower = jnp.where(y < 2, 1.0, 0.0)
     own0 = own_term(0)
     ut0[y % 2, x] = ut0[y % 2, x] + own0 * lower
     c0a = send(ut0.at[0:2, :, other, :], b0c.at[0:2], sibling)
-    advance(0)
     arrive(x2s)
     b2s[...] = b2c[x] + b2x[0] + b2x[1] + b2x[2]
     z2s = z_stage(b2s, b2z)
+    advance(2)
+    advance(0)
     node_terms(0, ut0, 4, 6)
-    advance(1)
     node_terms(0, ut0, 6, 8)
     ut0[2 + y % 2, x] = ut0[2 + y % 2, x] + own0 * (1.0 - lower)
     c0b = send(ut0.at[2:4, :, other, :], b0c.at[2:4], sibling)
+    advance(1)
 
     def add_rows(first):
         def step(i, carry):
@@ -393,7 +401,6 @@
     add_rows(0)
     arrive([c0b])
     add_rows(2)
-    mid = LANES // 2
     y0s = y_send(lambda to: b0c.at[to, :, 0:mid, :], b0y)
     x0s = x_send(lambda to: b0c.at[:, to, mid:LANES, :], b0x)
     advance(2)
@@ -401,14 +408,20 @@
     r2 = z_sum(b2s, b2z, z2s)
     g2[x] = r2
     a2 = [send(g2.at[x], g2.at[x], device(xs(a), y, z, c)) for a in X_PEERS]
-    advance(1)
     arrive(x1s)
     for i in range(2):
-        b1s[i] = b1c[x * 2 + i] + b1x[0, i] + b1x[1, i] + b1x[2, i]
-    y1s = send(b1s.at[1 - yy], b1y, device(x, partner, z, c))
+        b1p[i] = b1c[x, i, 0:mid, :] + b1x[0, i] + b1x[1, i] + b1x[2, i]
+    y1t = send(b1p.at[1 - yy], b1v, device(x, partner, z, c))
+    arrive([y1s])
+    for i in range(NX):
+        b1q[i] = b1c[i, yy, mid:LANES, :] + b1y[i]
+    x1t = x_send(lambda to: b1q.at[to], b1u)
+    advance(1)
     work(1)
-    arrive([y1s])
-    b1t[...] = b1s[yy] + b1y[...]
+    arrive([y1t])
+    b1t[0:mid, :] = b1p[yy] + b1v[...]
+    arrive(x1t)
+    b1t[mid:LANES, :] = b1q[x] + b1u[0] + b1u[1] + b1u[2]
     z1s = z_stage(b1t, b1z)
     advance(0)
 
@@ -587,12 +600,13 @@
         pltpu.VMEM((LOC, LOC), F32), pltpu.VMEM((RHS, LOC), F32), pltpu.VMEM((RHS, LOC), F32),
         pltpu.VMEM((2 * RHS, 1792), BF16), pltpu.VMEM((1792, LOC), BF16), pltpu.VMEM((1792, LOC), BF16),
         pltpu.VMEM((3584, LOC), BF16), pltpu.VMEM((3584, LOC), BF16),
-        piece(4, 4, rows=RHS), piece(8, rows=RHS), piece(4, rows=RHS),
+        piece(4, 4, rows=RHS), piece(4, 2, rows=RHS), piece(4, rows=RHS),
         pltpu.VMEM((NZ, 2, BLK, WIDE), F32),
         piece(16, rows=RHS), piece(8, rows=RHS), piece(4, rows=RHS),
-        piece(4, rows=LANES), piece(8, rows=LANES), piece(4, 4, rows=LANES),
+        piece(4, rows=LANES), piece(4, 2, rows=LANES), piece(4, 4, rows=LANES),
         piece(3, rows=LANES), piece(rows=LANES), piece(7),
-        piece(3, 2, rows=LANES), piece(2, rows=LANES), piece(rows=LANES), piece(rows=LANES), piece(7),
+        piece(3, 2, rows=64), piece(4, rows=64), piece(2, rows=64), piece(4, rows=64),
+        piece(3, rows=64), piece(rows=64), piece(rows=LANES), piece(7),
         piece(3, 4, rows=64), piece(3, 4, rows=64), piece(4, rows=64), piece(4, rows=64),
         piece(3, rows=64), piece(3, rows=64), piece(rows=LANES), piece(7),
         piece(4), piece(8), piece(7), piece(8), piece(16), piece(15), piece(16),
@@ -613,11 +627,34 @@
     )(*operands)
 
 
+def copy_kernel(first, second, first_out, second_out, sems):
+    moves = [
+        pltpu.make_async_copy(first, first_out, sems.at[0]),
+        pltpu.make_async_copy(second, second_out, sems.at[1]),
+    ]
+    for move in moves:
+        move.start()
+    for move in moves:
+        move.wait()
+
+
+def hand_on(*results):
+    hbm = pl.BlockSpec(memory_space=pl.ANY)
+    return pl.pallas_call(
+        copy_kernel,
+        out_shape=[jax.ShapeDtypeStruct(result.shape, F32) for result in results],
+        in_specs=[hbm] * 2,
+        out_specs=[hbm] * 2,
+        scratch_shapes=[pltpu.SemaphoreType.DMA((2,))],
+        compiler_params=pltpu.CompilerParams(vmem_limit_bytes=58 * 1024 * 1024),
+    )(*results)
+
+
 def body(rhs_sub, rhs_sep, sub_factor, sub_diag, sep_factor, sep_diag, sub_update, update_rows, sep_update):
     result_sub, result_sep = whole(
         sub_diag, update_rows, rhs_sep, sep_factor, sep_diag, sep_update[0].T, sub_factor[0], rhs_sub[0], sub_update[0]
     )
-    return result_sub[None], result_sep
+    return hand_on(result_sub[None], result_sep)
 
 
 def solution(mesh):

time: 106 us -> 118 us (1.11); the launches traced: 105 us -> 118 us
  Pallas kernels: 101 us -> 117 us
  local copies, waits for them, and re-layouts: 3.21 us -> 0 us
    pallas_call x0 -> x1, Pallas kernels: none -> 17.7 us  [hand_on(): pl.pallas_call(copy_kernel, out_shape=[jax.ShapeDtypeStruct(result.shape,...]
    unnamed x2 -> x0, local copies, waits for them, and re-layouts: 3.21 us -> none
    pallas_call x1, Pallas kernels: 101 us -> 99.4 us  [whole(): pl.pallas_call(whole_kernel, out_shape=[jax.ShapeDtypeStruct((LOC, RHS),...]
where the time goes in v5:
time: 118 us
  Pallas kernels  117 us (99%)
    pallas_call x1, Pallas kernels, whole(): pl.pallas_call(whole_kernel, out_shape=[jax.ShapeDtypeStruct((LOC, RHS),...  99.4 us
    pallas_call x1, Pallas kernels, hand_on(): pl.pallas_call(copy_kernel, out_shape=[jax.ShapeDtypeStruct(result.shape,...  17.7 us

profile of v5, /device:TPU:1, one launch (start us, length us, event | category | flops | bytes accessed | tf_op | source)
XLA Modules:
  0.0 118.0 jit_solution(3246587268754108540)
XLA Ops:
  0.6 99.4 %shard_map.104 = (f32[512,256]{1,0:T(8,128)}, f32[3,8,256]{2,1,0:T(8,128)}) custom-call(f32[1,512]{1,0:T(1,128)} %diag.1, s32[1,1792]{1,0:T(1,128)} %rows.1, f32[3,8,256]{2,1,0:T(8,128)} %rhs_sep.1, f32[8,3584]{1,0:T(8,128)} %sep_factor.1, f32[3,8]{1,0:T(4,128)} %sep_diag.1, f32[8,5120]{1,0:T(8,128)} %bitcast.11, f32[512,512]{1,0:T(8,128)} %bitcast.8, ...), custom_call_target="tpu_custom_call" | custom-call | tf_op jit(solution)/shard_map/pallas_call | solution.py:618
  100.0 17.7 %shard_map.105 = (f32[1,512,256]{2,1,0:T(8,128)}, f32[3,8,256]{2,1,0:T(8,128)}) custom-call(f32[1,512,256]{2,1,0:T(8,128)} %bitcast.9, f32[3,8,256]{2,1,0:T(8,128)} %get-tuple-element.5.second), custom_call_target="tpu_custom_call" | custom-call | tf_op jit(solution)/shard_map/pallas_call | solution.py:643

commit v6 on v5

--- a/solution.py
+++ b/solution.py
@@ -32,7 +32,7 @@
 
 def small_dot(left, right, dims):
     left_high, left_low = split(left)
-    right_high, right_low = split(right)
+    right_high, right_low = right if isinstance(right, tuple) else split(right)
     rows = left.shape[0]
     both = jnp.concatenate([left_high, left_low], axis=0)
     first = lax.dot_general(both, right_high, dims, preferred_element_type=F32)
@@ -58,6 +58,9 @@
 Z_PEERS = (4, 3, 5, 2, 6, 1, 7)
 PLANE = sorted(
     [(a, b) for a in range(NX) for b in range(NY)][1:], key=lambda ab: -hops(ab[0], NX) - hops(ab[1], NY)
+)
+SIDE = sorted(
+    [(a, d) for a in range(NX) for d in range(NZ)][1:], key=lambda ad: -hops(ad[0], NX) - hops(ad[1], NZ)
 )
 HALF = sorted([(a, b) for a in range(NX) for b in range(2)][1:], key=lambda ab: -hops(ab[0], NX) - ab[1])
 ROUNDS = ((0, 1536), (1536, 4608), (4608, 8704))
@@ -155,7 +158,7 @@
     diag, rows, rhs_sep, sep_factor, sep_diag, turned, factor_hbm, rhs_hbm, update_hbm,
     out_sub, out_sep,
     factor, rhs, update, inverse, solved_t, current, terms, update_high, update_low, moved_high, moved_low,
-    ut0, ut1, ut2, m_ref, x0, x1, x2,
+    ut0, ut1, ut2, m_ref, m_high, m_low, x0, x1, x2,
     b2c, b1c, b0c, b2x, b2s, b2z, b1x, b1y, b1p, b1q, b1u, b1v, b1t, b1z, b0y, b0x, b0p, b0q, b0u, b0v, b0t, b0z,
     g2, p1, p1r, g1, p0, p0r, g0, q0, q0r, h0, q1, q1r, h1, q2, q2r, h2,
     lsem, ssem, rsem,
@@ -186,7 +189,7 @@
 
     barrier = pltpu.get_barrier_semaphore()
     greeted = [device(xs(a), ys(b), z, c) for a, b in PLANE]
-    greeted += [device(x, y, zs(d), c) for d in range(1, NZ)] + [sibling]
+    greeted += [device(xs(a), y, zs(d), c) for a, d in SIDE if d > 0] + [sibling]
     for peer in greeted:
         pl.semaphore_signal(barrier, inc=1, device_id=peer, device_id_type=MESH)
 
@@ -381,13 +384,12 @@
     arrive(x2s)
     b2s[...] = b2c[x] + b2x[0] + b2x[1] + b2x[2]
     z2s = z_stage(b2s, b2z)
+    node_terms(0, ut0, 4, 6)
     advance(2)
-    advance(0)
-    node_terms(0, ut0, 4, 6)
     node_terms(0, ut0, 6, 8)
     ut0[2 + y % 2, x] = ut0[2 + y % 2, x] + own0 * (1.0 - lower)
     c0b = send(ut0.at[2:4, :, other, :], b0c.at[2:4], sibling)
-    advance(1)
+    advance(0)
 
     def add_rows(first):
         def step(i, carry):
@@ -399,10 +401,12 @@
 
     arrive([c0a])
     add_rows(0)
+    x0s = x_send(lambda to: b0c.at[0:2, to, mid:LANES, :], b0x.at[:, 0:2])
     arrive([c0b])
     add_rows(2)
     y0s = y_send(lambda to: b0c.at[to, :, 0:mid, :], b0y)
-    x0s = x_send(lambda to: b0c.at[:, to, mid:LANES, :], b0x)
+    x0s += x_send(lambda to: b0c.at[2:4, to, mid:LANES, :], b0x.at[:, 2:4])
+    advance(1)
     advance(2)
     advance(0)
     r2 = z_sum(b2s, b2z, z2s)
@@ -433,7 +437,15 @@
             ref[i] = value[:, i * LANES : (i + 1) * LANES]
 
     def columns(start, size):
-        return m_ref[:, :, :, start : start + size].reshape(LANES, size)
+        return m_high[:, start : start + size], m_low[:, start : start + size]
+
+    def unpack(turn):
+        arrive(shared[turn])
+        start, stop = ROUNDS[turn]
+        for at in range(start, stop, 512):
+            high, low = split(m_ref[:, :, :, at : at + 512].reshape(LANES, 512))
+            m_high[:, at : at + 512] = high
+            m_low[:, at : at + 512] = low
 
     here1 = yy * NX + x
     here0 = y * NX + x
@@ -467,7 +479,7 @@
 
     arrive(a2)
     advance(2)
-    arrive(shared[0])
+    unpack(0)
     solved2 = small_dot(joined(g2), columns(G2, 512), NT)
     spill(small_dot(solved2, columns(E21, 1024), NN), p1)
     p1s = scatter_half(p1, p1r)
@@ -484,7 +496,7 @@
     r1 = z_sum(b1t, b1z, z1s)
     g1[here1] = r1 - s1_scale * summed(p1, here1, p1r, p1s)
     a1 = gather_half(g1)
-    arrive(shared[1])
+    unpack(1)
     up0 = small_dot(solved2, columns(E20, 2048), NN)
     advance(2)
     arrive(x0t)
@@ -494,7 +506,7 @@
     z0s = z_stage(b0t, b0z)
     arrive(a1)
     solved1 = small_dot(joined(g1), columns(G1, 1024), NT)
-    arrive(shared[2])
+    unpack(2)
     spill(up0 + small_dot(solved1, columns(E10, 2048), NN), p0)
     p0s = scatter_plane(p0, p0r)
     work(2)
@@ -546,13 +558,12 @@
         send(x0.at[8:16, high, :], x0.at[8:16, high, :], device(x, y, zs(6), c)),
     ]
     h2[x] = summed(q2, x, q2r, q2s)
-    z2h = along_z(h2, x, x2)
+    x2[x, spread, :] = h2[x]
+    z2h = [send(h2.at[x], x2.at[x, spread, :], device(xs(a), y, zs(d), c)) for a, d in SIDE]
     arrive(z1h)
     w1 = [send(x1.at[here1, mine, :], x1.at[here1, mine, :], device(xs(a), pair_y(b), z, c)) for a, b in HALF]
     work(99)
     arrive(near0)
-    arrive(z2h)
-    w2 = [send(x2.at[x, mine, :], x2.at[x, mine, :], device(xs(a), y, z, c)) for a in X_PEERS]
 
     def swap_cores(result, batch):
         arrive(batch)
@@ -578,9 +589,9 @@
         )
 
     w0 = swap_cores(x0, far0)
+    w1 = swap_cores(x1, w1)
     take_in(0, x0, w0)
-    w1 = swap_cores(x1, w1)
-    w2 = swap_cores(x2, w2)
+    w2 = swap_cores(x2, z2h)
     take_in(1, x1, w1)
     take_in(2, x2, w2)
     out_sub[...] = small_dot(current[...] * scale, inverse[...], NN).T
@@ -588,7 +599,7 @@
         copy.wait_send()
 
 
-N_COPIES = 256
+N_COPIES = 320
 
 
 def whole(*operands):
@@ -601,7 +612,7 @@
         pltpu.VMEM((2 * RHS, 1792), BF16), pltpu.VMEM((1792, LOC), BF16), pltpu.VMEM((1792, LOC), BF16),
         pltpu.VMEM((3584, LOC), BF16), pltpu.VMEM((3584, LOC), BF16),
         piece(4, 4, rows=RHS), piece(4, 2, rows=RHS), piece(4, rows=RHS),
-        pltpu.VMEM((NZ, 2, BLK, WIDE), F32),
+        pltpu.VMEM((NZ, 2, BLK, WIDE), F32), pltpu.VMEM((LANES, WIDE), BF16), pltpu.VMEM((LANES, WIDE), BF16),
         piece(16, rows=RHS), piece(8, rows=RHS), piece(4, rows=RHS),
         piece(4, rows=LANES), piece(4, 2, rows=LANES), piece(4, 4, rows=LANES),
         piece(3, rows=LANES), piece(rows=LANES), piece(7),
@@ -627,25 +638,18 @@
     )(*operands)
 
 
-def copy_kernel(first, second, first_out, second_out, sems):
-    moves = [
-        pltpu.make_async_copy(first, first_out, sems.at[0]),
-        pltpu.make_async_copy(second, second_out, sems.at[1]),
-    ]
-    for move in moves:
-        move.start()
-    for move in moves:
-        move.wait()
+def copy_kernel(first, second, first_out, second_out):
+    first_out[...] = first[...]
+    second_out[...] = second[...]
 
 
 def hand_on(*results):
-    hbm = pl.BlockSpec(memory_space=pl.ANY)
+    vmem = pl.BlockSpec(memory_space=pltpu.VMEM)
     return pl.pallas_call(
         copy_kernel,
         out_shape=[jax.ShapeDtypeStruct(result.shape, F32) for result in results],
-        in_specs=[hbm] * 2,
-        out_specs=[hbm] * 2,
-        scratch_shapes=[pltpu.SemaphoreType.DMA((2,))],
+        in_specs=[vmem] * 2,
+        out_specs=[vmem] * 2,
         compiler_params=pltpu.CompilerParams(vmem_limit_bytes=58 * 1024 * 1024),
     )(*results)
 

time: 118 us -> 103 us (0.87)
  Pallas kernels: 117 us -> 102 us
    pallas_call x1, Pallas kernels: 17.7 us -> 1.87 us  [hand_on(): pl.pallas_call(copy_kernel, out_shape=[jax.ShapeDtypeStruct(result.shape,...]
where the time goes in v6:
time: 103 us
  Pallas kernels  102 us (99%)
    pallas_call x1, Pallas kernels, whole(): pl.pallas_call(whole_kernel, out_shape=[jax.ShapeDtypeStruct((LOC, RHS),...  100 us

profile of v6, /device:TPU:1, one launch (start us, length us, event | category | flops | bytes accessed | tf_op | source)
XLA Modules:
  0.0 102.9 jit_solution(1634106220008915346)
XLA Ops:
  0.6 100.4 %shard_map.104 = (f32[512,256]{1,0:T(8,128)}, f32[3,8,256]{2,1,0:T(8,128)}) custom-call(f32[1,512]{1,0:T(1,128)} %diag.1, s32[1,1792]{1,0:T(1,128)} %rows.1, f32[3,8,256]{2,1,0:T(8,128)} %rhs_sep.1, f32[8,3584]{1,0:T(8,128)} %sep_factor.1, f32[3,8]{1,0:T(4,128)} %sep_diag.1, f32[8,5120]{1,0:T(8,128)} %bitcast.11, f32[512,512]{1,0:T(8,128)} %bitcast.8, ...), custom_call_target="tpu_custom_call" | custom-call | tf_op jit(solution)/shard_map/pallas_call | solution.py:629
  101.0 1.9 %shard_map.105 = (f32[1,512,256]{2,1,0:T(8,128)}, f32[3,8,256]{2,1,0:T(8,128)}) custom-call(f32[1,512,256]{2,1,0:T(8,128)} %bitcast.9, f32[3,8,256]{2,1,0:T(8,128)} %get-tuple-element.5.second), custom_call_target="tpu_custom_call" | custom-call | tf_op jit(solution)/shard_map/pallas_call | solution.py:648

commit v7 on v6

--- a/solution.py
+++ b/solution.py
@@ -146,18 +146,17 @@
     blocks = [piece[:, i : i + 512] for piece in pieces for i in range(0, piece.shape[1], 512)]
     stacked = jnp.concatenate(blocks, axis=0)
     swap = jnp.where(reorder(iota((512, 512), 0)) == iota((512, 512), 1), 1.0, 0.0).astype(BF16)
-    high, middle, low = split3(stacked)
-    return (
-        jnp.dot(high, swap, preferred_element_type=F32)
-        + jnp.dot(middle, swap, preferred_element_type=F32)
-        + jnp.dot(low, swap, preferred_element_type=F32)
-    )
+    count = stacked.shape[0]
+    exact = jnp.concatenate([part.astype(F32) for part in split3(stacked)], axis=0).astype(BF16)
+    moved = jnp.dot(exact, swap, preferred_element_type=F32)
+    return moved[:count] + moved[count : 2 * count] + moved[2 * count :]
 
 
 def whole_kernel(
     diag, rows, rhs_sep, sep_factor, sep_diag, turned, factor_hbm, rhs_hbm, update_hbm,
     out_sub, out_sep,
     factor, rhs, update, inverse, solved_t, current, terms, update_high, update_low, moved_high, moved_low,
+    inverse_high, inverse_low,
     ut0, ut1, ut2, m_ref, m_high, m_low, x0, x1, x2,
     b2c, b1c, b0c, b2x, b2s, b2z, b1x, b1y, b1p, b1q, b1u, b1v, b1t, b1z, b0y, b0x, b0p, b0q, b0u, b0v, b0t, b0z,
     g2, p1, p1r, g1, p0, p0r, g0, q0, q0r, h0, q1, q1r, h1, q2, q2r, h2,
@@ -209,17 +208,16 @@
         for copy in batch:
             copy.wait_recv()
 
+    loads[0].wait()
+    loads[1].wait()
     own_rows = separator_rows(sep_factor, sep_diag, turned, position)
     for i in range(WIDE // 512):
         m_ref[z, c, :, i * 512 : (i + 1) * 512] = own_rows[i * BLK : (i + 1) * BLK]
 
     scale = 1.0 / diag[...]
-    loads[0].wait()
     invert(factor, scale, inverse)
-    loads[1].wait()
     right_t = rhs[...].T
     solved_t[...] = small_dot(right_t, inverse[...], NT) * scale
-    current[...] = solved_t[...]
 
     pl.semaphore_wait(barrier, len(greeted))
 
@@ -341,8 +339,11 @@
                 listed = slice(sub_start(level), sub_start(level) + count)
                 at = slice(row_start(level) + i * 256, row_start(level) + i * 256 + 256)
                 pick = chosen(level, i)
-                moved_high[at, :] = jnp.dot(pick, update_high[listed, :], preferred_element_type=F32).astype(BF16)
-                moved_low[at, :] = jnp.dot(pick, update_low[listed, :], preferred_element_type=F32).astype(BF16)
+                entries = jnp.dot(pick, update_high[listed, :], preferred_element_type=F32)
+                entries = entries + jnp.dot(pick, update_low[listed, :], preferred_element_type=F32)
+                high, low = split(small_dot(entries * scale, (inverse_high[...], inverse_low[...]), NN))
+                moved_high[at, :] = high
+                moved_low[at, :] = low
 
     def x_send(piece, landed):
         return [send(piece(xs(a)), landed.at[a - 1], device(xs(a), y, z, c)) for a in X_PEERS]
@@ -363,7 +364,7 @@
     c1 = send(ut1.at[:, :, other, :], b1c, sibling)
     advance(0)
     coupling_terms(0)
-    mid = LANES // 2
+    mid, mid0 = LANES // 2, 48
     arrive([c1])
 
     def add_pair(i, carry):
@@ -401,11 +402,11 @@
 
     arrive([c0a])
     add_rows(0)
-    x0s = x_send(lambda to: b0c.at[0:2, to, mid:LANES, :], b0x.at[:, 0:2])
+    x0s = x_send(lambda to: b0c.at[0:2, to, mid0:LANES, :], b0x.at[:, 0:2])
     arrive([c0b])
     add_rows(2)
-    y0s = y_send(lambda to: b0c.at[to, :, 0:mid, :], b0y)
-    x0s += x_send(lambda to: b0c.at[2:4, to, mid:LANES, :], b0x.at[:, 2:4])
+    y0s = y_send(lambda to: b0c.at[to, :, 0:mid0, :], b0y)
+    x0s += x_send(lambda to: b0c.at[2:4, to, mid0:LANES, :], b0x.at[:, 2:4])
     advance(1)
     advance(2)
     advance(0)
@@ -421,6 +422,9 @@
         b1q[i] = b1c[i, yy, mid:LANES, :] + b1y[i]
     x1t = x_send(lambda to: b1q.at[to], b1u)
     advance(1)
+    high, low = split(inverse[...])
+    inverse_high[...] = high
+    inverse_low[...] = low
     work(1)
     arrive([y1t])
     b1t[0:mid, :] = b1p[yy] + b1v[...]
@@ -487,11 +491,11 @@
     work(1)
     arrive(y0s)
     for i in range(NX):
-        b0p[i] = b0c[y, i, 0:mid, :] + b0y[0, i] + b0y[1, i] + b0y[2, i]
+        b0p[i] = b0c[y, i, 0:mid0, :] + b0y[0, i] + b0y[1, i] + b0y[2, i]
     x0t = x_send(lambda to: b0p.at[to], b0u)
     arrive(x0s)
     for i in range(NY):
-        b0q[i] = b0c[i, x, mid:LANES, :] + b0x[0, i] + b0x[1, i] + b0x[2, i]
+        b0q[i] = b0c[i, x, mid0:LANES, :] + b0x[0, i] + b0x[1, i] + b0x[2, i]
     y0t = y_send(lambda to: b0q.at[to], b0v)
     r1 = z_sum(b1t, b1z, z1s)
     g1[here1] = r1 - s1_scale * summed(p1, here1, p1r, p1s)
@@ -500,9 +504,9 @@
     up0 = small_dot(solved2, columns(E20, 2048), NN)
     advance(2)
     arrive(x0t)
-    b0t[0:mid, :] = b0p[x] + b0u[0] + b0u[1] + b0u[2]
+    b0t[0:mid0, :] = b0p[x] + b0u[0] + b0u[1] + b0u[2]
     arrive(y0t)
-    b0t[mid:LANES, :] = b0q[y] + b0v[0] + b0v[1] + b0v[2]
+    b0t[mid0:LANES, :] = b0q[y] + b0v[0] + b0v[1] + b0v[2]
     z0s = z_stage(b0t, b0z)
     arrive(a1)
     solved1 = small_dot(joined(g1), columns(G1, 1024), NT)
@@ -513,12 +517,22 @@
     r0 = z_sum(b0t, b0z, z0s)
     g0[here0] = r0 - s0_scale * summed(p0, here0, p0r, p0s)
     a0 = gather_plane(g0)
-    work(2)
+    work(3)
     arrive(a0)
     solved0 = small_dot(joined(g0), columns(G0, 2048), NT)
 
     def block_of(d):
         return pl.ds(pl.multiple_of(c * LANES + zs(d) * COLS, COLS), COLS)
+
+    def first_leg(ds):
+        return [send(h0, x0.at[:, spread, :], device(x, y, zs(d), c)) for d in ds]
+
+    def second_leg():
+        arrive(far0)
+        low, high = x0.at[:, block_of(6), :], x0.at[:, block_of(2), :]
+        first, second = x0.at[0:8, block_of(6), :], x0.at[8:16, block_of(2), :]
+        steps = ((low, 1), (high, 7), (first, 2), (second, 6))
+        return [send(part, part, device(x, y, zs(d), c)) for part, d in steps]
 
     def along_z(chunk, at, result):
         result[at, spread, :] = chunk[at]
@@ -529,12 +543,11 @@
     work(2)
     h0[here0] = summed(q0, here0, q0r, q0s)
     a0 = gather_plane(h0)
-    work(2)
+    work(3)
     arrive(a0)
     x0[:, spread, :] = h0[...]
-    far0, near0 = [
-        [send(h0, x0.at[:, spread, :], device(x, y, zs(d), c)) for d in ds] for ds in ((2, 6), (1, 7))
-    ]
+    far0 = first_leg((2, 6))
+    near0 = first_leg((1, 7))
     found0 = joined(h0)
     y1 = solved1 - s0_scale * small_dot(found0, columns(E10, 2048), NT)
     spill(small_dot(y1, columns(G1, 1024), NN), q1)
@@ -544,57 +557,58 @@
     h1[here1] = summed(q1, here1, q1r, q1s)
     a1 = gather_half(h1)
     z1h = along_z(h1, here1, x1)
-    work(2)
+    work(1)
     arrive(a1)
     y2 = y2 - s1_scale * small_dot(joined(h1), columns(E21, 1024), NT)
     spill(small_dot(y2, columns(G2, 512), NN), q2)
     q2s = x_send(lambda to: q2.at[to], q2r)
-    arrive(far0)
-    low, high = block_of(6), block_of(2)
-    far0 = [
-        send(x0.at[:, low, :], x0.at[:, low, :], device(x, y, zs(1), c)),
-        send(x0.at[:, high, :], x0.at[:, high, :], device(x, y, zs(7), c)),
-        send(x0.at[0:8, low, :], x0.at[0:8, low, :], device(x, y, zs(2), c)),
-        send(x0.at[8:16, high, :], x0.at[8:16, high, :], device(x, y, zs(6), c)),
-    ]
+    near0 += second_leg()
+    arrive(z1h)
+    w1s = [send(x1.at[here1, mine, :], x1.at[here1, mine, :], device(xs(a), pair_y(b), z, c)) for a, b in HALF]
     h2[x] = summed(q2, x, q2r, q2s)
     x2[x, spread, :] = h2[x]
     z2h = [send(h2.at[x], x2.at[x, spread, :], device(xs(a), y, zs(d), c)) for a, d in SIDE]
-    arrive(z1h)
-    w1 = [send(x1.at[here1, mine, :], x1.at[here1, mine, :], device(xs(a), pair_y(b), z, c)) for a, b in HALF]
     work(99)
-    arrive(near0)
+    current[...] = small_dot(solved_t[...] * scale, (inverse_high[...], inverse_low[...]), NN)
 
     def swap_cores(result, batch):
         arrive(batch)
         return send(result.at[:, mine, :], result.at[:, mine, :], sibling)
 
-    def take_in(level, result, copy):
-        arrive([copy])
-
+    def product(result, i, half, first, second):
+        both = jnp.concatenate([result[2 * i, half, :], result[2 * i + 1, half, :]], axis=1)
+        return small_dot(both, (first, second), NN)
+
+    def take_in(level, result, half):
         def step(i, carry):
             at = pl.ds(pl.multiple_of(row_start(level) + i * 256, 256), 256)
-            both = jnp.concatenate([result[2 * i], result[2 * i + 1]], axis=1)
-            high, low = split(both)
-            stacked = jnp.concatenate([high, low], axis=0)
-            first = jnp.dot(stacked, moved_high[at, :], preferred_element_type=F32)
-            second = jnp.dot(high, moved_low[at, :], preferred_element_type=F32)
-            current[...] = current[...] - weight_scale(level) * (first[:RHS] + first[RHS:] + second)
+            total = product(result, i, half, moved_high[at, :], moved_low[at, :])
+            current[half, :] = current[half, :] - weight_scale(level) * total
             return carry
 
         lax.fori_loop(0, (ROWS >> level) // 256, step, 0)
-        chunk = [here0, here1, x][level]
+
+    def own_result(level, result, chunk):
         out_sep[level] = lax.dot_general(
             mark, result[chunk], NT, precision=lax.Precision.HIGHEST, preferred_element_type=F32
         )
 
-    w0 = swap_cores(x0, far0)
-    w1 = swap_cores(x1, w1)
-    take_in(0, x0, w0)
+    w0 = swap_cores(x0, near0)
+    w1 = swap_cores(x1, w1s)
+    take_in(0, x0, mine)
     w2 = swap_cores(x2, z2h)
-    take_in(1, x1, w1)
-    take_in(2, x2, w2)
-    out_sub[...] = small_dot(current[...] * scale, inverse[...], NN).T
+    take_in(1, x1, mine)
+    arrive([w0])
+    take_in(0, x0, other)
+    own_result(0, x0, here0)
+    arrive([w1])
+    take_in(1, x1, other)
+    own_result(1, x1, here1)
+    take_in(2, x2, mine)
+    arrive([w2])
+    take_in(2, x2, other)
+    out_sub[...] = current[...].T
+    own_result(2, x2, x)
     for copy in copies:
         copy.wait_send()
 
@@ -611,6 +625,7 @@
         pltpu.VMEM((LOC, LOC), F32), pltpu.VMEM((RHS, LOC), F32), pltpu.VMEM((RHS, LOC), F32),
         pltpu.VMEM((2 * RHS, 1792), BF16), pltpu.VMEM((1792, LOC), BF16), pltpu.VMEM((1792, LOC), BF16),
         pltpu.VMEM((3584, LOC), BF16), pltpu.VMEM((3584, LOC), BF16),
+        pltpu.VMEM((LOC, LOC), BF16), pltpu.VMEM((LOC, LOC), BF16),
         piece(4, 4, rows=RHS), piece(4, 2, rows=RHS), piece(4, rows=RHS),
         pltpu.VMEM((NZ, 2, BLK, WIDE), F32), pltpu.VMEM((LANES, WIDE), BF16), pltpu.VMEM((LANES, WIDE), BF16),
         piece(16, rows=RHS), piece(8, rows=RHS), piece(4, rows=RHS),
@@ -618,8 +633,8 @@
         piece(3, rows=LANES), piece(rows=LANES), piece(7),
         piece(3, 2, rows=64), piece(4, rows=64), piece(2, rows=64), piece(4, rows=64),
         piece(3, rows=64), piece(rows=64), piece(rows=LANES), piece(7),
-        piece(3, 4, rows=64), piece(3, 4, rows=64), piece(4, rows=64), piece(4, rows=64),
-        piece(3, rows=64), piece(3, rows=64), piece(rows=LANES), piece(7),
+        piece(3, 4, rows=48), piece(3, 4, rows=80), piece(4, rows=48), piece(4, rows=80),
+        piece(3, rows=48), piece(3, rows=80), piece(rows=LANES), piece(7),
         piece(4), piece(8), piece(7), piece(8), piece(16), piece(15), piece(16),
         piece(16), piece(15), piece(16), piece(8), piece(7), piece(8), piece(4), piece(3), piece(4),
         pltpu.SemaphoreType.DMA((3,)), pltpu.SemaphoreType.DMA((N_COPIES,)), pltpu.SemaphoreType.DMA((N_COPIES,)),

time: 103 us -> 101 us (0.981)
  Pallas kernels: 102 us -> 100 us
    pallas_call x1, Pallas kernels: 100 us -> 98.3 us  [whole(): pl.pallas_call(whole_kernel, out_shape=[jax.ShapeDtypeStruct((LOC, RHS),...]
where the time goes in v7:
time: 101 us
  Pallas kernels  100 us (99%)
    pallas_call x1, Pallas kernels, whole(): pl.pallas_call(whole_kernel, out_shape=[jax.ShapeDtypeStruct((LOC, RHS),...  98.3 us

profile of v7, /device:TPU:1, one launch (start us, length us, event | category | flops | bytes accessed | tf_op | source)
XLA Modules:
  0.0 100.8 jit_solution(8458706214818454172)
XLA Ops:
  0.6 98.3 %shard_map.104 = (f32[512,256]{1,0:T(8,128)}, f32[3,8,256]{2,1,0:T(8,128)}) custom-call(f32[1,512]{1,0:T(1,128)} %diag.1, s32[1,1792]{1,0:T(1,128)} %rows.1, f32[3,8,256]{2,1,0:T(8,128)} %rhs_sep.1, f32[8,3584]{1,0:T(8,128)} %sep_factor.1, f32[3,8]{1,0:T(4,128)} %sep_diag.1, f32[8,5120]{1,0:T(8,128)} %bitcast.11, f32[512,512]{1,0:T(8,128)} %bitcast.8, ...), custom_call_target="tpu_custom_call" | custom-call | tf_op jit(solution)/shard_map/pallas_call | solution.py:644
  98.9 1.9 %shard_map.105 = (f32[1,512,256]{2,1,0:T(8,128)}, f32[3,8,256]{2,1,0:T(8,128)}) custom-call(f32[1,512,256]{2,1,0:T(8,128)} %bitcast.9, f32[3,8,256]{2,1,0:T(8,128)} %get-tuple-element.5.second), custom_call_target="tpu_custom_call" | custom-call | tf_op jit(solution)/shard_map/pallas_call | solution.py:663

commit v8 on v7

--- a/solution.py
+++ b/solution.py
@@ -403,16 +403,6 @@
     arrive([c0a])
     add_rows(0)
     x0s = x_send(lambda to: b0c.at[0:2, to, mid0:LANES, :], b0x.at[:, 0:2])
-    arrive([c0b])
-    add_rows(2)
-    y0s = y_send(lambda to: b0c.at[to, :, 0:mid0, :], b0y)
-    x0s += x_send(lambda to: b0c.at[2:4, to, mid0:LANES, :], b0x.at[:, 2:4])
-    advance(1)
-    advance(2)
-    advance(0)
-    r2 = z_sum(b2s, b2z, z2s)
-    g2[x] = r2
-    a2 = [send(g2.at[x], g2.at[x], device(xs(a), y, z, c)) for a in X_PEERS]
     arrive(x1s)
     for i in range(2):
         b1p[i] = b1c[x, i, 0:mid, :] + b1x[0, i] + b1x[1, i] + b1x[2, i]
@@ -421,7 +411,16 @@
     for i in range(NX):
         b1q[i] = b1c[i, yy, mid:LANES, :] + b1y[i]
     x1t = x_send(lambda to: b1q.at[to], b1u)
+    arrive([c0b])
+    add_rows(2)
+    y0s = y_send(lambda to: b0c.at[to, :, 0:mid0, :], b0y)
+    x0s += x_send(lambda to: b0c.at[2:4, to, mid0:LANES, :], b0x.at[:, 2:4])
     advance(1)
+    r2 = z_sum(b2s, b2z, z2s)
+    g2[x] = r2
+    a2 = [send(g2.at[x], g2.at[x], device(xs(a), y, z, c)) for a in X_PEERS]
+    advance(2)
+    advance(0)
     high, low = split(inverse[...])
     inverse_high[...] = high
     inverse_low[...] = low
@@ -431,6 +430,7 @@
     arrive(x1t)
     b1t[mid:LANES, :] = b1q[x] + b1u[0] + b1u[1] + b1u[2]
     z1s = z_stage(b1t, b1z)
+    advance(1)
     advance(0)
 
     def joined(ref):
@@ -600,11 +600,11 @@
     take_in(1, x1, mine)
     arrive([w0])
     take_in(0, x0, other)
-    own_result(0, x0, here0)
     arrive([w1])
     take_in(1, x1, other)
+    take_in(2, x2, mine)
+    own_result(0, x0, here0)
     own_result(1, x1, here1)
-    take_in(2, x2, mine)
     arrive([w2])
     take_in(2, x2, other)
     out_sub[...] = current[...].T

time: 101 us -> 101 us (level)
  no operation moved by 1% of the time
where the time goes in v8:
time: 101 us; the launch traced here: 99.9 us
  Pallas kernels  99.3 us (98%)
    pallas_call x1, Pallas kernels, whole(): pl.pallas_call(whole_kernel, out_shape=[jax.ShapeDtypeStruct((LOC, RHS),...  97.4 us

profile of v8, /device:TPU:1, one launch (start us, length us, event | category | flops | bytes accessed | tf_op | source)
XLA Modules:
  0.0 99.9 jit_solution(18182859448693218745)
XLA Ops:
  0.6 97.4 %shard_map.104 = (f32[512,256]{1,0:T(8,128)}, f32[3,8,256]{2,1,0:T(8,128)}) custom-call(f32[1,512]{1,0:T(1,128)} %diag.1, s32[1,1792]{1,0:T(1,128)} %rows.1, f32[3,8,256]{2,1,0:T(8,128)} %rhs_sep.1, f32[8,3584]{1,0:T(8,128)} %sep_factor.1, f32[3,8]{1,0:T(4,128)} %sep_diag.1, f32[8,5120]{1,0:T(8,128)} %bitcast.11, f32[512,512]{1,0:T(8,128)} %bitcast.8, ...), custom_call_target="tpu_custom_call" | custom-call | tf_op jit(solution)/shard_map/pallas_call | solution.py:644
  98.0 1.9 %shard_map.105 = (f32[1,512,256]{2,1,0:T(8,128)}, f32[3,8,256]{2,1,0:T(8,128)}) custom-call(f32[1,512,256]{2,1,0:T(8,128)} %bitcast.9, f32[3,8,256]{2,1,0:T(8,128)} %get-tuple-element.5.second), custom_call_target="tpu_custom_call" | custom-call | tf_op jit(solution)/shard_map/pallas_call | solution.py:663
